TPU v7x, 32 devices: a whole 2x2x4 slice. The times are simulated.
32 devices in a mesh: groups: 2 (over x), rows: 16 (over z, y, core).
Axes of the slice: x: 2, y: 2, z: 4, core: 2. Of those that a mesh axis runs over, the one named last changes fastest.
Arguments:
- row_leaves: int32 [32, 65536], P(None, ('groups', 'rows')), parts along dimension 1, may hold values from 0 to 127
- covariates: bfloat16 [64, 65536], P(None, ('groups', 'rows')), parts along dimension 1, may hold values from -6 to 6
- query_leaves: int32 [32, 128], P(None, 'groups'), parts along dimension 1, may hold values from 0 to 127
- leaf_sizes: int32 [64, 128], P('groups'), parts along dimension 0, may hold values from 128 to 511
Outputs:
- moments: float32 [128, 4096], P(('groups', 'rows')), parts along dimension 0
There are 2 independent parts, one for each index of `groups`. A program takes and returns all parts, laid end to end along the dimension named above; each array names one. Nothing has to cross between parts.
All inputs are finite; a program needn't handle non-finite values.
Results may differ from a plain program's by a relative error of at most 0.0006.
Values may be sent and summed in bfloat16 or wider, within the bound.
No kernel may reach another device: no remote copies, remote signals or barrier semaphores. Data moves between devices by JAX's collectives and lax.ppermute only.
A program may use at most 64 MiB of HBM per device.

v0:
```python
import math

import jax
import jax.numpy as jnp
from jax import lax
from jax.sharding import PartitionSpec as P


def moment_rows(covar_block):
    widened = covar_block.astype(jnp.float32)
    width, amount = widened.shape
    product = (widened[:, None, :] * widened[None, :, :]).reshape(width * width, amount)
    return product.astype(jnp.bfloat16)


def query_table(query_leaves, leaf_sizes, amount):
    trees, leaves = leaf_sizes.shape
    inverse = 1.0 / (trees * leaf_sizes.astype(jnp.float32))
    hits = query_leaves.T[:, :, None] == jnp.arange(leaves, dtype=jnp.int32)[None, None, :]
    table = jnp.where(hits, inverse[None, :, :], jnp.float32(0.0)).astype(jnp.bfloat16)
    return table.reshape(amount, trees * leaves)


def kernel_weights(table, leaf_block):
    trees, amount = leaf_block.shape
    leaves = table.shape[1] // trees
    one_hot = (leaf_block[:, None, :] == jnp.arange(leaves, dtype=jnp.int32)[None, :, None]).astype(
        jnp.bfloat16
    )
    one_hot = one_hot.reshape(trees * leaves, amount)
    return jnp.dot(table, one_hot, preferred_element_type=jnp.float32).astype(jnp.bfloat16)


def contract(weights, product):
    return lax.dot_general(
        weights, product, (((1,), (1,)), ((), ())), preferred_element_type=jnp.float32
    )


def per_device(row_leaves, covariates, query_leaves, leaf_sizes):
    width = covariates.shape[0]
    columns = width * width
    local_rows = covariates.shape[1]
    all_queries = query_leaves.shape[1]
    query_dev = all_queries // lax.axis_size("rows")
    row_block = math.gcd(local_rows, 256)
    count_blocks = local_rows // row_block
    table = query_table(query_leaves, leaf_sizes, query_dev * lax.axis_size("rows"))

    def step(position, running):
        first_row = position * row_block
        leaf_block = lax.dynamic_slice_in_dim(row_leaves, first_row, row_block, 1)
        covar_block = lax.dynamic_slice_in_dim(covariates, first_row, row_block, 1)
        weights = kernel_weights(table, leaf_block)
        return running + contract(weights, moment_rows(covar_block))

    return lax.psum_scatter(
        lax.fori_loop(
            0,
            count_blocks,
            step,
            jnp.zeros((query_dev * lax.axis_size("rows"), columns), jnp.float32),
        ),
        "rows",
        scatter_dimension=0,
        tiled=True,
    )


def solution(mesh):
    return jax.shard_map(
        per_device,
        mesh=mesh,
        in_specs=(
            P(None, ("groups", "rows")),
            P(None, ("groups", "rows")),
            P(None, "groups"),
            P("groups", None),
        ),
        out_specs=P(("groups", "rows"), None),
        check_vma=False,
    )
```

profile of v0, /device:TPU:0, one launch (start us, length us, event | category | flops | bytes accessed | tf_op | source)
XLA Modules:
  0.0 189.5 jit_solution(1931076621658625831)
XLA Ops:
  6.5 0.8 copy.6
  8.1 76.8 %while.14 = (s32[]{:T(128)}, f32[64,4096]{1,0:T(8,128)}, s32[32,2048]{1,0:T(8,128)}, bf16[64,2048]{1,0:T(8,128)(2,1)}, s32[64,32]{1,0:T(8,128)S(1)}, /*index=5*/...) while((s32[]{:T(128)}, f32[64,4096]{1,0:T(8,128)}, ...), condition=%wide.region_1.2_spmd.clone, body=%wide.region_0.1_spmd.clone.sunk | while | flops 273711104 | bytes 12910765 | solution.py:58
  8.1 0.8 dynamic-slice_convert_fusion.2
  9.6 0.8 constant_dynamic-slice_fusion.3
  10.3 1.7 fusion.18
  12.4 5.1 %convolution_add_fusion.2 = f32[64,4096]{1,0:T(8,128)} fusion(bf16[4096,256]{1,0:T(8,128)(2,1)S(1)} %bitcast.36, bf16[4096,256]{1,0:T(8,128)(2,1)} %fusion.18, f32[64,4096]{1,0:T(8,128)} %get-tuple-element.198, s32[8,8,32,128]{3,2,1,0:T(8,128)S(1)} %bitcast.37, bf16[4096]{0:T(1024)(128)(2,1)S(1)} %get-tuple-element.214, ...), kind=kOutput, calls=%fused_computation.1.clone.1 | convolution fusion | flops 269500416 | bytes 7364609 | tf_op jit(solution)/shard_map/while/body/eval_jaxpr/dot_general | solution.py:35
  17.5 0.8 dynamic-slice_convert_fusion.2
  18.9 0.8 constant_dynamic-slice_fusion.3
  19.7 1.7 fusion.18
  21.7 5.4 %convolution_add_fusion.2 = f32[64,4096]{1,0:T(8,128)} fusion(bf16[4096,256]{1,0:T(8,128)(2,1)S(1)} %bitcast.36, bf16[4096,256]{1,0:T(8,128)(2,1)} %fusion.18, f32[64,4096]{1,0:T(8,128)} %get-tuple-element.198, s32[8,8,32,128]{3,2,1,0:T(8,128)S(1)} %bitcast.37, bf16[4096]{0:T(1024)(128)(2,1)S(1)} %get-tuple-element.214, ...), kind=kOutput, calls=%fused_computation.1.clone.1 | convolution fusion | flops 269500416 | bytes 7364609 | tf_op jit(solution)/shard_map/while/body/eval_jaxpr/dot_general | solution.py:35
  27.1 0.8 dynamic-slice_convert_fusion.2
  28.5 0.8 constant_dynamic-slice_fusion.3
  29.3 1.7 fusion.18
  31.4 5.4 %convolution_add_fusion.2 = f32[64,4096]{1,0:T(8,128)} fusion(bf16[4096,256]{1,0:T(8,128)(2,1)S(1)} %bitcast.36, bf16[4096,256]{1,0:T(8,128)(2,1)} %fusion.18, f32[64,4096]{1,0:T(8,128)} %get-tuple-element.198, s32[8,8,32,128]{3,2,1,0:T(8,128)S(1)} %bitcast.37, bf16[4096]{0:T(1024)(128)(2,1)S(1)} %get-tuple-element.214, ...), kind=kOutput, calls=%fused_computation.1.clone.1 | convolution fusion | flops 269500416 | bytes 7364609 | tf_op jit(solution)/shard_map/while/body/eval_jaxpr/dot_general | solution.py:35
  36.7 0.8 dynamic-slice_convert_fusion.2
  38.2 0.8 constant_dynamic-slice_fusion.3
  38.9 1.7 fusion.18
  41.0 5.4 %convolution_add_fusion.2 = f32[64,4096]{1,0:T(8,128)} fusion(bf16[4096,256]{1,0:T(8,128)(2,1)S(1)} %bitcast.36, bf16[4096,256]{1,0:T(8,128)(2,1)} %fusion.18, f32[64,4096]{1,0:T(8,128)} %get-tuple-element.198, s32[8,8,32,128]{3,2,1,0:T(8,128)S(1)} %bitcast.37, bf16[4096]{0:T(1024)(128)(2,1)S(1)} %get-tuple-element.214, ...), kind=kOutput, calls=%fused_computation.1.clone.1 | convolution fusion | flops 269500416 | bytes 7364609 | tf_op jit(solution)/shard_map/while/body/eval_jaxpr/dot_general | solution.py:35
  47.8 0.8 constant_dynamic-slice_fusion.3
  48.6 1.7 fusion.18
  50.6 5.4 %convolution_add_fusion.2 = f32[64,4096]{1,0:T(8,128)} fusion(bf16[4096,256]{1,0:T(8,128)(2,1)S(1)} %bitcast.36, bf16[4096,256]{1,0:T(8,128)(2,1)} %fusion.18, f32[64,4096]{1,0:T(8,128)} %get-tuple-element.198, s32[8,8,32,128]{3,2,1,0:T(8,128)S(1)} %bitcast.37, bf16[4096]{0:T(1024)(128)(2,1)S(1)} %get-tuple-element.214, ...), kind=kOutput, calls=%fused_computation.1.clone.1 | convolution fusion | flops 269500416 | bytes 7364609 | tf_op jit(solution)/shard_map/while/body/eval_jaxpr/dot_general | solution.py:35
  57.4 0.8 constant_dynamic-slice_fusion.3
  58.2 1.7 fusion.18
  60.2 5.4 %convolution_add_fusion.2 = f32[64,4096]{1,0:T(8,128)} fusion(bf16[4096,256]{1,0:T(8,128)(2,1)S(1)} %bitcast.36, bf16[4096,256]{1,0:T(8,128)(2,1)} %fusion.18, f32[64,4096]{1,0:T(8,128)} %get-tuple-element.198, s32[8,8,32,128]{3,2,1,0:T(8,128)S(1)} %bitcast.37, bf16[4096]{0:T(1024)(128)(2,1)S(1)} %get-tuple-element.214, ...), kind=kOutput, calls=%fused_computation.1.clone.1 | convolution fusion | flops 269500416 | bytes 7364609 | tf_op jit(solution)/shard_map/while/body/eval_jaxpr/dot_general | solution.py:35
  67.0 0.8 constant_dynamic-slice_fusion.3
  67.8 1.7 fusion.18
  69.9 5.4 %convolution_add_fusion.2 = f32[64,4096]{1,0:T(8,128)} fusion(bf16[4096,256]{1,0:T(8,128)(2,1)S(1)} %bitcast.36, bf16[4096,256]{1,0:T(8,128)(2,1)} %fusion.18, f32[64,4096]{1,0:T(8,128)} %get-tuple-element.198, s32[8,8,32,128]{3,2,1,0:T(8,128)S(1)} %bitcast.37, bf16[4096]{0:T(1024)(128)(2,1)S(1)} %get-tuple-element.214, ...), kind=kOutput, calls=%fused_computation.1.clone.1 | convolution fusion | flops 269500416 | bytes 7364609 | tf_op jit(solution)/shard_map/while/body/eval_jaxpr/dot_general | solution.py:35
  76.7 0.8 constant_dynamic-slice_fusion.3
  77.4 1.7 fusion.18
  79.5 5.4 %convolution_add_fusion.2 = f32[64,4096]{1,0:T(8,128)} fusion(bf16[4096,256]{1,0:T(8,128)(2,1)S(1)} %bitcast.36, bf16[4096,256]{1,0:T(8,128)(2,1)} %fusion.18, f32[64,4096]{1,0:T(8,128)} %get-tuple-element.198, s32[8,8,32,128]{3,2,1,0:T(8,128)S(1)} %bitcast.37, bf16[4096]{0:T(1024)(128)(2,1)S(1)} %get-tuple-element.214, ...), kind=kOutput, calls=%fused_computation.1.clone.1 | convolution fusion | flops 269500416 | bytes 7364609 | tf_op jit(solution)/shard_map/while/body/eval_jaxpr/dot_general | solution.py:35
  86.1 95.0 %all-reduce.3.cloned.1.call-done = f32[64,4096]{1,0:T(8,128)} async-done(((f32[64,4096]{1,0:T(8,128)}), f32[64,4096]{1,0:T(8,128)}) %all-reduce.3.cloned.1.call-update) | async-done | bytes 1048592
  181.1 1.5 constant_dynamic-slice_fusion.1
  (36 shorter events, 12.5 us)
Async XLA Ops:
  6.5 174.6 %all-reduce.3.cloned.1.call-start = ((), (), s32[]{:S(2)}) async-start(), calls=%async_computation | async-start | bytes 2097152
  8.1 76.8 %copy-start = (u32[32]{0:T(128)S(1)}, u32[32]{0:T(128)}, u32[]{:S(2)}) copy-start(u32[32]{0:T(128)} %constant.39) | copy-start | bytes 388
Sparse Core Ops, SparseCore 0:
  85.0 96.0 all-reduce.2
where the time goes:
time: 191 us; the launch traced here: 189 us
  waiting for transfers between devices  95 us (50%)
  matrix products  42.6 us (22%)
  other arithmetic  26 us (14%)
  between operations  14.1 us (7%)
  local copies, waits for them, and re-layouts  11.7 us (6%)
    unnamed x2, waiting for transfers between devices  95 us
    dot_general x8, matrix products, contract(): lax.dot_general(weights, product, (((1,), (1,)), ((), ())), preferred_ele...  42.6 us
    while x8, other arithmetic  13.7 us
    dynamic_slice x8, local copies, waits for them, and re-layouts, step(): leaf_block = lax.dynamic_slice_in_dim(row_leaves, first_row, row_block, 1)  6.14 us
    convert_element_type x8, other arithmetic, moment_rows(): widened = covar_block.astype(jnp.float32)  6.11 us
    convert_element_type x8, other arithmetic, moment_rows(): return product.astype(jnp.bfloat16)  5.45 us
  transfers between devices with their start and end apart: 1, of which 1 were waited for; matrix products, arithmetic and copies ran while one was open for 0% of the time, Pallas kernels for 0%

commit v1 on v0

v1 whole, which is shorter than its diff:
```python
import functools
import math

import jax
import jax.numpy as jnp
from jax import lax
from jax.experimental import pallas as pl
from jax.experimental.pallas import tpu as pltpu
from jax.sharding import PartitionSpec as P

SUB = 8
LANES = 128
NT = (((1,), (1,)), ((), ()))


def segments(width):
    found, offset = [], 0
    for j in range(width):
        first = j // SUB * SUB
        found.append((offset, first))
        offset += width - first
    return found, offset


def stages(count):
    bits = [1 << i for i in range(count.bit_length() - 1)]
    rest = bits[1:]
    return [bits[:1]] * (count > 1) + [rest[i : i + 2] for i in range(0, len(rest), 2)]


def block_order(count):
    order = [0]
    for group in reversed(stages(count)):
        shifts = [sum(b for i, b in enumerate(group) if (s >> i) & 1) for s in range(1 << len(group))]
        order = [s | p for s in shifts for p in order]
    return order


def moments_kernel(axis, order, unit, rl_ref, x_ref, ql_ref, ls_ref, *out_refs):
    trees, rows = rl_ref.shape
    width = x_ref.shape[0]
    queries = ql_ref.shape[1]
    share = queries // len(order)
    me = lax.axis_index(axis)

    span = max(queries, LANES)
    place = lax.broadcasted_iota(jnp.int32, (trees, span), 1)
    block = jnp.zeros((trees, span), jnp.int32)
    for i in range(len(order).bit_length() - 1):
        block += ((place // share >> i) & 1) * order[1 << i]
    source = ((block ^ me) * share + place % share) % queries
    leaves = ql_ref[...]
    if queries < span:
        leaves = jnp.concatenate([leaves] * (span // queries), axis=1)
    inverse = 1.0 / (trees * ls_ref[...].astype(jnp.float32))
    leaf_parts, weight_parts = [], []
    for part in range(span // LANES):
        at = source[:, part * LANES : (part + 1) * LANES]
        taken = jnp.zeros((trees, LANES), jnp.int32)
        for piece in range(span // LANES):
            got = jnp.take_along_axis(leaves[:, piece * LANES : (piece + 1) * LANES], at % LANES, axis=1)
            taken = jnp.where(at // LANES == piece, got, taken)
        weight = jnp.take_along_axis(inverse, taken, axis=1).astype(jnp.bfloat16).astype(jnp.float32)
        leaf_parts.append(taken.T)
        weight_parts.append((weight.T * unit).astype(jnp.int32))
    leaf = jnp.concatenate(leaf_parts, 0)[:queries].astype(jnp.int16)
    weight = jnp.concatenate(weight_parts, 0)[:queries].astype(jnp.int16)

    step, tall = 256, 32
    for start in range(0, rows, step):
        here = slice(start, start + step)
        row_leaf = rl_ref[:, here].astype(jnp.int16)
        parts = []
        for top in range(0, queries, tall):
            total = jnp.zeros((tall, step), jnp.int16)
            for b in range(trees):
                want = jnp.broadcast_to(leaf[top : top + tall, b : b + 1], (tall, step))
                gives = jnp.broadcast_to(weight[top : top + tall, b : b + 1], (tall, step))
                have = jnp.broadcast_to(row_leaf[b : b + 1], (tall, step))
                total += jnp.where(have == want, gives, jnp.int16(0))
            parts.append((total.astype(jnp.float32) * (1.0 / unit)).astype(jnp.bfloat16))
        kernel_weight = jnp.concatenate(parts, 0)
        wide = x_ref[:, here].astype(jnp.float32)
        row_moments = jnp.concatenate([wide[j : j + 1] * wide[j // SUB * SUB :] for j in range(width)], 0)
        row_moments = row_moments.astype(jnp.bfloat16)
        product = lax.dot_general(kernel_weight, row_moments, NT, preferred_element_type=jnp.float32)
        top = 0
        for ref in out_refs:
            piece = product[top : top + ref.shape[0]]
            ref[...] = piece if start == 0 else ref[...] + piece
            top += ref.shape[0]


def expand_kernel(width, first_ref, second_ref, out_ref, held, full):
    share = out_ref.shape[0]
    total = first_ref[...] + second_ref[...]
    where, _ = segments(width)
    for j in range(width):
        offset, first = where[j]
        held[j, :, first:width] = total[:, offset : offset + width - first]
    upper = lax.broadcasted_iota(jnp.int32, (width, width), 1) >= lax.broadcasted_iota(
        jnp.int32, (width, width), 0
    )
    for q in range(share):
        square = held[:, q, :width]
        full[:, q, :width] = jnp.where(upper, square, square.T)
    for j in range(width):
        out_ref[:, j * width : (j + 1) * width] = full[j, :, :width]


def per_device(row_leaves, covariates, query_leaves, leaf_sizes):
    axis = "rows"
    count = lax.axis_size(axis)
    trees, local_rows = row_leaves.shape
    width = covariates.shape[0]
    queries = query_leaves.shape[1]
    leaves = leaf_sizes.shape[1]
    share = queries // count
    _, columns = segments(width)
    least = local_rows * count // leaves // 2
    unit = float(trees * least * 512)
    order = block_order(count)
    groups = stages(count)

    half = queries // 2
    held, sent = pl.pallas_call(
        functools.partial(moments_kernel, axis, order, unit),
        out_shape=[jax.ShapeDtypeStruct((half, columns), jnp.float32)] * 2,
        compiler_params=pltpu.CompilerParams(vmem_limit_bytes=40 << 20),
        cost_estimate=pl.CostEstimate(
            flops=2 * queries * columns * local_rows,
            bytes_accessed=1 << 20,
            transcendentals=0,
        ),
        name="moments",
    )(row_leaves, covariates, query_leaves, leaf_sizes)

    def permute(array, shift):
        return lax.ppermute(array, axis, [(i, i ^ shift) for i in range(count)])

    first, second = held, permute(sent, groups[0][0])
    for group in groups[1:]:
        total = first + second
        blocks = 1 << len(group)
        size = total.shape[0] // blocks
        arrived = []
        for s in range(1, blocks):
            shift = sum(b for i, b in enumerate(group) if (s >> i) & 1)
            arrived.append(permute(total[s * size : (s + 1) * size], shift))
        first = total[:size]
        for extra in arrived[:-1]:
            first = first + extra
        second = arrived[-1]

    return pl.pallas_call(
        functools.partial(expand_kernel, width),
        out_shape=jax.ShapeDtypeStruct((share, width * width), jnp.float32),
        scratch_shapes=[pltpu.VMEM((width, share, LANES), jnp.float32)] * 2,
        name="expand",
    )(first, second)


def solution(mesh):
    return jax.shard_map(
        per_device,
        mesh=mesh,
        in_specs=(
            P(None, ("groups", "rows")),
            P(None, ("groups", "rows")),
            P(None, "groups"),
            P("groups", None),
        ),
        out_specs=P(("groups", "rows"), None),
        check_vma=False,
    )
```

time: 191 us -> 26.1 us (0.14)
  waiting for transfers between devices: 95 us -> 7.76 us
  matrix products: 42.6 us -> 0 us
  other arithmetic: 26 us -> 0.07 us
  between operations: 14.1 us -> 0.03 us
  starting transfers between devices: 0.01 us -> 7.65 us
  local copies, waits for them, and re-layouts: 11.7 us -> 4.58 us
  Pallas kernels: 0 us -> 5.72 us
    unnamed x2 -> x0, waiting for transfers between devices: 95 us -> none
    dot_general x8 -> x0, matrix products: 42.6 us -> none  [contract(): lax.dot_general(weights, product, (((1,), (1,)), ((), ())), preferred_ele...]
    while x8 -> x0, other arithmetic: 13.7 us -> none
    convert_element_type x16 -> x0, other arithmetic: 11.6 us -> none  [the longest x8 6.11 us: moment_rows(): widened = covar_block.astype(jnp.float32)]
    ppermute x0 -> x5, waiting for transfers between devices: none -> 7.76 us  [permute(): return lax.ppermute(array, axis, [(i, i ^ shift) for i in range(count)])]
    ppermute x0 -> x5, starting transfers between devices: none -> 7.65 us  [permute(): return lax.ppermute(array, axis, [(i, i ^ shift) for i in range(count)])]
    dynamic_slice x8 -> x0, local copies, waits for them, and re-layouts: 6.14 us -> none  [step(): leaf_block = lax.dynamic_slice_in_dim(row_leaves, first_row, row_block, 1)]
    pallas_call x0 -> x2, Pallas kernels: none -> 5.72 us  [the longest x1 3.87 us: per_device(): pl.pallas_call(functools.partial(moments_kernel, axis, order, unit), out_...]
  transfers between devices with their start and end apart: 1 -> 5, of which waited for: 1 -> 4; matrix products, arithmetic and copies ran while one was open for 0% -> 0% of each run, Pallas kernels for 0% -> 0%
where the time goes in v1:
time: 26.1 us; the launch traced here: 25.8 us
  waiting for transfers between devices  7.76 us (30%)
  starting transfers between devices  7.65 us (29%)
  Pallas kernels  5.72 us (22%)
  local copies, waits for them, and re-layouts  4.58 us (18%)
    ppermute x5, waiting for transfers between devices, permute(): return lax.ppermute(array, axis, [(i, i ^ shift) for i in range(count)])  7.76 us
    ppermute x5, starting transfers between devices, permute(): return lax.ppermute(array, axis, [(i, i ^ shift) for i in range(count)])  7.65 us
    unnamed x10, local copies, waits for them, and re-layouts  3.94 us
    pallas_call x1, Pallas kernels, per_device(): pl.pallas_call(functools.partial(moments_kernel, axis, order, unit), out_...  3.87 us
    pallas_call x1, Pallas kernels, per_device(): pl.pallas_call(functools.partial(expand_kernel, width), out_shape=jax.Sha...  1.84 us
    slice x2, local copies, waits for them, and re-layouts, per_device(): arrived.append(permute(total[s * size:(s + 1) * size], shift))  0.64 us
  transfers between devices with their start and end apart: 5, of which 4 were waited for; matrix products, arithmetic and copies ran while one was open for 0% of the time, Pallas kernels for 0%

profile of v1, /device:TPU:0, one launch (start us, length us, event | category | flops | bytes accessed | tf_op | source)
XLA Modules:
  0.0 25.8 jit_solution(12226298050225073425)
XLA Ops:
  0.0 0.0 copy-start
  0.0 0.9 %copy-done = s32[32,2048]{1,0:T(8,128)S(1)} copy-done((s32[32,2048]{1,0:T(8,128)S(1)}, s32[32,2048]{1,0:T(8,128)}, u32[]{:S(2)}) %copy-start) | copy-done | bytes 262168
  1.0 0.0 copy-start.1
  1.0 0.9 %copy-done.1 = bf16[64,2048]{1,0:T(8,128)(2,1)S(1)} copy-done((bf16[64,2048]{1,0:T(8,128)(2,1)S(1)}, bf16[64,2048]{1,0:T(8,128)(2,1)}, u32[]{:S(2)}) %copy-start.1) | copy-done | bytes 262168
  1.9 0.0 copy-start.2
  1.9 0.7 %copy-done.2 = s32[32,64]{1,0:T(8,128)S(1)} copy-done((s32[32,64]{1,0:T(8,128)S(1)}, s32[32,64]{1,0:T(8,128)}, u32[]{:S(2)}) %copy-start.2) | copy-done | bytes 8216
  2.6 0.0 copy-start.3
  2.6 0.7 %copy-done.3 = s32[32,128]{1,0:T(8,128)S(1)} copy-done((s32[32,128]{1,0:T(8,128)S(1)}, s32[32,128]{1,0:T(8,128)}, u32[]{:S(2)}) %copy-start.3) | copy-done | bytes 16408
  3.3 3.9 %moments.1 = (f32[32,2304]{1,0:T(8,128)S(1)}, f32[32,2304]{1,0:T(8,128)S(1)}) custom-call(s32[32,2048]{1,0:T(8,128)S(1)} %copy-done, bf16[64,2048]{1,0:T(8,128)(2,1)S(1)} %copy-done.1, s32[32,64]{1,0:T(8,128)S(1)} %copy-done.2, s32[32,128]{1,0:T(8,128)S(1)} %copy-done.3), custom_call_target="tpu_custom_call" | custom-call | flops 603979776 | bytes 1048576 | tf_op jit(solution)/shard_map/moments/pallas_call | solution.py:126
  7.2 0.5 %collective-permute-start = (f32[32,2304]{1,0:T(8,128)S(1)}, f32[32,2304]{1,0:T(8,128)S(1)}, u32[]{:S(2)}, u32[]{:S(2)}) collective-permute-start(f32[32,2304]{1,0:T(8,128)S(1)} %get-tuple-element.8), channel_id=1, source_target_pairs={{0,1},{1,0},{2,3},{3,2},{4,5},{5,4},{6,7},{7,6},{8,9},{9,8},{10,11... | collective-permute-start | bytes 884744 | tf_op jit(solution)/shard_map/ppermute | solution.py:139
  7.7 1.2 %collective-permute-done = f32[32,2304]{1,0:T(8,128)S(1)} collective-permute-done((f32[32,2304]{1,0:T(8,128)S(1)}, f32[32,2304]{1,0:T(8,128)S(1)}, u32[]{:S(2)}, u32[]{:S(2)}) %collective-permute-start) | collective-permute-done | bytes 294944 | tf_op jit(solution)/shard_map/ppermute | solution.py:139
  9.0 3.0 %collective-permute-start.1 = (f32[8,2304]{1,0:T(8,128)S(1)}, f32[8,2304]{1,0:T(8,128)S(1)}, u32[]{:S(2)}, u32[]{:S(2)}) collective-permute-start(f32[8,2304]{1,0:T(8,128)S(1)} %get-tuple-element.9), channel_id=1, source_target_pairs={{0,2},{1,3},{2,0},{3,1},{4,6},{5,7},{6,4},{7,5},{8,10},{9,11},{10,... | collective-permute-start | bytes 221192 | tf_op jit(solution)/shard_map/ppermute | solution.py:139
  12.0 1.5 %collective-permute-start.3 = (f32[8,2304]{1,0:T(8,128)S(1)}, f32[8,2304]{1,0:T(8,128)S(1)}, u32[]{:S(2)}, u32[]{:S(2)}) collective-permute-start(f32[8,2304]{1,0:T(8,128)S(1)} %get-tuple-element.10), channel_id=1, source_target_pairs={{0,6},{1,7},{2,4},{3,5},{4,2},{5,3},{6,0},{7,1},{8,14},{9,15},{10,... | collective-permute-start | bytes 221192 | tf_op jit(solution)/shard_map/ppermute | solution.py:139
  13.5 0.1 collective-permute-start.2
  13.6 1.9 %collective-permute-done.1 = f32[8,2304]{1,0:T(8,128)S(1)} collective-permute-done((f32[8,2304]{1,0:T(8,128)S(1)}, f32[8,2304]{1,0:T(8,128)S(1)}, u32[]{:S(2)}, u32[]{:S(2)}) %collective-permute-start.1) | collective-permute-done | bytes 73760 | tf_op jit(solution)/shard_map/ppermute | solution.py:139
  15.5 2.4 %collective-permute-done.3 = f32[8,2304]{1,0:T(8,128)S(1)} collective-permute-done((f32[8,2304]{1,0:T(8,128)S(1)}, f32[8,2304]{1,0:T(8,128)S(1)}, u32[]{:S(2)}, u32[]{:S(2)}) %collective-permute-start.3) | collective-permute-done | bytes 73760 | tf_op jit(solution)/shard_map/ppermute | solution.py:139
  17.8 0.0 collective-permute-done.2
  17.9 0.6 %fusion.3 = (f32[4,2304]{1,0:T(4,128)S(1)}, f32[4,2304]{1,0:T(4,128)}) fusion(f32[8,2304]{1,0:T(8,128)S(1)} %fusion.1), kind=kLoop, calls=%fused_computation.4 | loop fusion | bytes 147456 | tf_op jit(solution)/shard_map/slice | solution.py:149
  18.5 2.6 %collective-permute-start.4 = (f32[4,2304]{1,0:T(4,128)S(1)}, f32[4,2304]{1,0:T(4,128)S(1)}, u32[]{:S(2)}, u32[]{:S(2)}) collective-permute-start(f32[4,2304]{1,0:T(4,128)S(1)} %get-tuple-element.12), channel_id=1, source_target_pairs={{0,8},{1,9},{2,10},{3,11},{4,12},{5,13},{6,14},{7,15},{8,0},{9,1},... | collective-permute-start | bytes 110600 | tf_op jit(solution)/shard_map/ppermute | solution.py:139
  21.1 2.3 %collective-permute-done.4.second_ref = f32[4,2304]{1,0:T(4,128)S(1)} collective-permute-done((f32[4,2304]{1,0:T(4,128)S(1)}, f32[4,2304]{1,0:T(4,128)S(1)}, u32[]{:S(2)}, u32[]{:S(2)}) %collective-permute-start.4) | collective-permute-done | bytes 36896 | tf_op jit(solution)/shard_map/ppermute | solution.py:139
  23.4 0.0 copy-start.4
  23.4 0.6 %copy-done.4 = f32[4,2304]{1,0:T(4,128)} copy-done((f32[4,2304]{1,0:T(4,128)}, f32[4,2304]{1,0:T(4,128)S(1)}, u32[]{:S(2)}) %copy-start.4) | copy-done | bytes 36888
  24.0 1.8 %expand.1 = f32[4,4096]{1,0:T(4,128)} custom-call(f32[4,2304]{1,0:T(4,128)} %get-tuple-element.13.first_ref, f32[4,2304]{1,0:T(4,128)} %copy-done.4), custom_call_target="tpu_custom_call" | custom-call | tf_op jit(solution)/shard_map/expand/pallas_call | solution.py:155
  (3 shorter events, 0.1 us)
Async XLA Ops:
  0.0 0.9 %copy-start = (s32[32,2048]{1,0:T(8,128)S(1)}, s32[32,2048]{1,0:T(8,128)}, u32[]{:S(2)}) copy-start(s32[32,2048]{1,0:T(8,128)} %rl_ref.1) | copy-start | bytes 786436
  1.0 0.9 %copy-start.1 = (bf16[64,2048]{1,0:T(8,128)(2,1)S(1)}, bf16[64,2048]{1,0:T(8,128)(2,1)}, u32[]{:S(2)}) copy-start(bf16[64,2048]{1,0:T(8,128)(2,1)} %x_ref.1) | copy-start | bytes 786436
  1.9 0.7 %copy-start.2 = (s32[32,64]{1,0:T(8,128)S(1)}, s32[32,64]{1,0:T(8,128)}, u32[]{:S(2)}) copy-start(s32[32,64]{1,0:T(8,128)} %ql_ref.1) | copy-start | bytes 24580
  2.6 0.7 %copy-start.3 = (s32[32,128]{1,0:T(8,128)S(1)}, s32[32,128]{1,0:T(8,128)}, u32[]{:S(2)}) copy-start(s32[32,128]{1,0:T(8,128)} %ls_ref.1) | copy-start | bytes 49156
  7.2 1.7 %collective-permute-start = (f32[32,2304]{1,0:T(8,128)S(1)}, f32[32,2304]{1,0:T(8,128)S(1)}, u32[]{:S(2)}, u32[]{:S(2)}) collective-permute-start(f32[32,2304]{1,0:T(8,128)S(1)} %get-tuple-element.8), channel_id=1, source_target_pairs={{0,1},{1,0},{2,3},{3,2},{4,5},{5,4},{6,7},{7,6},{8,9},{9,8},{10,11... | collective-permute-start | bytes 884744 | tf_op jit(solution)/shard_map/ppermute | solution.py:139
  9.0 6.4 %collective-permute-start.1 = (f32[8,2304]{1,0:T(8,128)S(1)}, f32[8,2304]{1,0:T(8,128)S(1)}, u32[]{:S(2)}, u32[]{:S(2)}) collective-permute-start(f32[8,2304]{1,0:T(8,128)S(1)} %get-tuple-element.9), channel_id=1, source_target_pairs={{0,2},{1,3},{2,0},{3,1},{4,6},{5,7},{6,4},{7,5},{8,10},{9,11},{10,... | collective-permute-start | bytes 221192 | tf_op jit(solution)/shard_map/ppermute | solution.py:139
  12.0 5.9 %collective-permute-start.3 = (f32[8,2304]{1,0:T(8,128)S(1)}, f32[8,2304]{1,0:T(8,128)S(1)}, u32[]{:S(2)}, u32[]{:S(2)}) collective-permute-start(f32[8,2304]{1,0:T(8,128)S(1)} %get-tuple-element.10), channel_id=1, source_target_pairs={{0,6},{1,7},{2,4},{3,5},{4,2},{5,3},{6,0},{7,1},{8,14},{9,15},{10,... | collective-permute-start | bytes 221192 | tf_op jit(solution)/shard_map/ppermute | solution.py:139
  13.5 4.4 %collective-permute-start.2 = (f32[8,2304]{1,0:T(8,128)S(1)}, f32[8,2304]{1,0:T(8,128)S(1)}, u32[]{:S(2)}, u32[]{:S(2)}) collective-permute-start(f32[8,2304]{1,0:T(8,128)S(1)} %get-tuple-element.11), channel_id=1, source_target_pairs={{0,4},{1,5},{2,6},{3,7},{4,0},{5,1},{6,2},{7,3},{8,12},{9,13},{10,... | collective-permute-start | bytes 221192 | tf_op jit(solution)/shard_map/ppermute | solution.py:139
  18.5 4.9 %collective-permute-start.4 = (f32[4,2304]{1,0:T(4,128)S(1)}, f32[4,2304]{1,0:T(4,128)S(1)}, u32[]{:S(2)}, u32[]{:S(2)}) collective-permute-start(f32[4,2304]{1,0:T(4,128)S(1)} %get-tuple-element.12), channel_id=1, source_target_pairs={{0,8},{1,9},{2,10},{3,11},{4,12},{5,13},{6,14},{7,15},{8,0},{9,1},... | collective-permute-start | bytes 110600 | tf_op jit(solution)/shard_map/ppermute | solution.py:139
  23.4 0.6 %copy-start.4 = (f32[4,2304]{1,0:T(4,128)}, f32[4,2304]{1,0:T(4,128)S(1)}, u32[]{:S(2)}) copy-start(f32[4,2304]{1,0:T(4,128)S(1)} %collective-permute-done.4.second_ref) | copy-start | bytes 110596

commit v2 on v1

--- a/solution.py
+++ b/solution.py
@@ -36,12 +36,31 @@
     return order
 
 
-def moments_kernel(axis, order, unit, rl_ref, x_ref, ql_ref, ls_ref, *out_refs):
+def moments_kernel(axis, order, unit, step, rl_hbm, x_hbm, ql_hbm, ls_hbm, *refs):
+    *out_refs, rl_ref, x_ref, ql_ref, ls_ref, small, large = refs
     trees, rows = rl_ref.shape
     width = x_ref.shape[0]
     queries = ql_ref.shape[1]
     share = queries // len(order)
     me = lax.axis_index(axis)
+
+    copies = [
+        pltpu.make_async_copy(ql_hbm, ql_ref, small.at[0]),
+        pltpu.make_async_copy(ls_hbm, ls_ref, small.at[1]),
+    ]
+    pairs = []
+    for n, start in enumerate(range(0, rows, step)):
+        here = slice(start, start + step)
+        pairs.append(
+            (
+                pltpu.make_async_copy(rl_hbm.at[:, here], rl_ref.at[:, here], large.at[n, 0]),
+                pltpu.make_async_copy(x_hbm.at[:, here], x_ref.at[:, here], large.at[n, 1]),
+            )
+        )
+    for copy in copies + [copy for pair in pairs for copy in pair]:
+        copy.start()
+    for copy in copies:
+        copy.wait()
 
     span = max(queries, LANES)
     place = lax.broadcasted_iota(jnp.int32, (trees, span), 1)
@@ -66,9 +85,11 @@
     leaf = jnp.concatenate(leaf_parts, 0)[:queries].astype(jnp.int16)
     weight = jnp.concatenate(weight_parts, 0)[:queries].astype(jnp.int16)
 
-    step, tall = 256, 32
-    for start in range(0, rows, step):
+    tall = 32
+    for n, start in enumerate(range(0, rows, step)):
         here = slice(start, start + step)
+        for copy in pairs[n]:
+            copy.wait()
         row_leaf = rl_ref[:, here].astype(jnp.int16)
         parts = []
         for top in range(0, queries, tall):
@@ -93,19 +114,22 @@
 
 def expand_kernel(width, first_ref, second_ref, out_ref, held, full):
     share = out_ref.shape[0]
-    total = first_ref[...] + second_ref[...]
+    total = first_ref[:share] + second_ref[...]
     where, _ = segments(width)
+    tall = held.shape[0] // width
     for j in range(width):
         offset, first = where[j]
-        held[j, :, first:width] = total[:, offset : offset + width - first]
+        held[j * tall : j * tall + share, first:width] = total[:, offset : offset + width - first]
     upper = lax.broadcasted_iota(jnp.int32, (width, width), 1) >= lax.broadcasted_iota(
         jnp.int32, (width, width), 0
     )
     for q in range(share):
-        square = held[:, q, :width]
-        full[:, q, :width] = jnp.where(upper, square, square.T)
+        square = held[pl.ds(q, width, stride=tall), :][:, :width]
+        whole = jnp.where(upper, square, square.T)
+        full[pl.ds(q, width, stride=tall), :] = jnp.concatenate([whole] * (LANES // width), axis=1)
     for j in range(width):
-        out_ref[:, j * width : (j + 1) * width] = full[j, :, :width]
+        lane = j * width % LANES
+        out_ref[:, j * width : (j + 1) * width] = full[j * tall : j * tall + share, lane : lane + width]
 
 
 def per_device(row_leaves, covariates, query_leaves, leaf_sizes):
@@ -123,9 +147,17 @@
     groups = stages(count)
 
     half = queries // 2
+    step = math.gcd(local_rows, 256)
+    arguments = [
+        pltpu.with_memory_space_constraint(a, pltpu.HBM)
+        for a in (row_leaves, covariates, query_leaves, leaf_sizes)
+    ]
     held, sent = pl.pallas_call(
-        functools.partial(moments_kernel, axis, order, unit),
-        out_shape=[jax.ShapeDtypeStruct((half, columns), jnp.float32)] * 2,
+        functools.partial(moments_kernel, axis, order, unit, step),
+        out_shape=[pltpu.VMEM((half, columns), jnp.float32)] * 2,
+        in_specs=[pl.BlockSpec(memory_space=pltpu.HBM)] * len(arguments),
+        scratch_shapes=[pltpu.VMEM(a.shape, a.dtype) for a in arguments]
+        + [pltpu.SemaphoreType.DMA((2,)), pltpu.SemaphoreType.DMA((local_rows // step, 2))],
         compiler_params=pltpu.CompilerParams(vmem_limit_bytes=40 << 20),
         cost_estimate=pl.CostEstimate(
             flops=2 * queries * columns * local_rows,
@@ -133,29 +165,30 @@
             transcendentals=0,
         ),
         name="moments",
-    )(row_leaves, covariates, query_leaves, leaf_sizes)
+    )(*arguments)
 
     def permute(array, shift):
         return lax.ppermute(array, axis, [(i, i ^ shift) for i in range(count)])
 
     first, second = held, permute(sent, groups[0][0])
     for group in groups[1:]:
-        total = first + second
+        total = first[: second.shape[0]] + second
         blocks = 1 << len(group)
         size = total.shape[0] // blocks
         arrived = []
         for s in range(1, blocks):
             shift = sum(b for i, b in enumerate(group) if (s >> i) & 1)
             arrived.append(permute(total[s * size : (s + 1) * size], shift))
-        first = total[:size]
+        first = total
         for extra in arrived[:-1]:
-            first = first + extra
+            first = first[:size] + extra
         second = arrived[-1]
 
     return pl.pallas_call(
         functools.partial(expand_kernel, width),
         out_shape=jax.ShapeDtypeStruct((share, width * width), jnp.float32),
-        scratch_shapes=[pltpu.VMEM((width, share, LANES), jnp.float32)] * 2,
+        scratch_shapes=[pltpu.VMEM((width * 8, LANES), jnp.float32)] * 2,
+        compiler_params=pltpu.CompilerParams(vmem_limit_bytes=4 << 20),
         name="expand",
     )(first, second)
 

time: 26.1 us -> 22.2 us (0.85)
  local copies, waits for them, and re-layouts: 4.58 us -> 0.03 us
  Pallas kernels: 5.72 us -> 6.42 us
    unnamed x10 -> x0, local copies, waits for them, and re-layouts: 3.94 us -> none
    pallas_call x1, Pallas kernels: 3.87 us -> 5.45 us  [per_device(): pl.pallas_call(functools.partial(moments_kernel, axis, order, unit, step)...]
    pallas_call x1, Pallas kernels: 1.84 us -> 0.97 us  [per_device(): pl.pallas_call(functools.partial(expand_kernel, width), out_shape=jax.Sha...]
    slice x2, local copies, waits for them, and re-layouts: 0.64 us -> 0.03 us  [per_device(): arrived.append(permute(total[s * size:(s + 1) * size], shift))]
where the time goes in v2:
time: 22.2 us; the launch traced here: 22 us
  waiting for transfers between devices  7.77 us (35%)
  starting transfers between devices  7.71 us (35%)
  Pallas kernels  6.42 us (29%)
    ppermute x5, waiting for transfers between devices, permute(): return lax.ppermute(array, axis, [(i, i ^ shift) for i in range(count)])  7.77 us
    ppermute x5, starting transfers between devices, permute(): return lax.ppermute(array, axis, [(i, i ^ shift) for i in range(count)])  7.71 us
    pallas_call x1, Pallas kernels, per_device(): pl.pallas_call(functools.partial(moments_kernel, axis, order, unit, step)...  5.45 us
    pallas_call x1, Pallas kernels, per_device(): pl.pallas_call(functools.partial(expand_kernel, width), out_shape=jax.Sha...  0.97 us
  transfers between devices with their start and end apart: 5, of which 4 were waited for; matrix products, arithmetic and copies ran while one was open for 0% of the time, Pallas kernels for 0%

profile of v2, /device:TPU:0, one launch (start us, length us, event | category | flops | bytes accessed | tf_op | source)
XLA Modules:
  0.0 22.0 jit_solution(17174931295356907692)
XLA Ops:
  0.0 5.4 %moments.1 = (f32[32,2304]{1,0:T(8,128)S(1)}, f32[32,2304]{1,0:T(8,128)S(1)}) custom-call(s32[32,2048]{1,0:T(8,128)} %rl_hbm.1, bf16[64,2048]{1,0:T(8,128)(2,1)} %x_hbm.1, s32[32,64]{1,0:T(8,128)} %ql_hbm.1, s32[32,128]{1,0:T(8,128)} %ls_hbm.1), custom_call_target="tpu_custom_call" | custom-call | flops 603979776 | bytes 1048576 | tf_op jit(solution)/shard_map/moments/pallas_call | solution.py:155
  5.5 0.5 %collective-permute-start = (f32[32,2304]{1,0:T(8,128)S(1)}, f32[32,2304]{1,0:T(8,128)S(1)}, u32[]{:S(2)}, u32[]{:S(2)}) collective-permute-start(f32[32,2304]{1,0:T(8,128)S(1)} %get-tuple-element.8), channel_id=1, source_target_pairs={{0,1},{1,0},{2,3},{3,2},{4,5},{5,4},{6,7},{7,6},{8,9},{9,8},{10,11... | collective-permute-start | bytes 884744 | tf_op jit(solution)/shard_map/ppermute | solution.py:171
  6.0 1.2 %collective-permute-done = f32[32,2304]{1,0:T(8,128)S(1)} collective-permute-done((f32[32,2304]{1,0:T(8,128)S(1)}, f32[32,2304]{1,0:T(8,128)S(1)}, u32[]{:S(2)}, u32[]{:S(2)}) %collective-permute-start) | collective-permute-done | bytes 294944 | tf_op jit(solution)/shard_map/ppermute | solution.py:171
  7.3 2.9 %collective-permute-start.1 = (f32[8,2304]{1,0:T(8,128)S(1)}, f32[8,2304]{1,0:T(8,128)S(1)}, u32[]{:S(2)}, u32[]{:S(2)}) collective-permute-start(f32[8,2304]{1,0:T(8,128)S(1)} %get-tuple-element.9), channel_id=1, source_target_pairs={{0,2},{1,3},{2,0},{3,1},{4,6},{5,7},{6,4},{7,5},{8,10},{9,11},{10,... | collective-permute-start | bytes 221192 | tf_op jit(solution)/shard_map/ppermute | solution.py:171
  10.2 1.5 %collective-permute-start.3 = (f32[8,2304]{1,0:T(8,128)S(1)}, f32[8,2304]{1,0:T(8,128)S(1)}, u32[]{:S(2)}, u32[]{:S(2)}) collective-permute-start(f32[8,2304]{1,0:T(8,128)S(1)} %get-tuple-element.10), channel_id=1, source_target_pairs={{0,6},{1,7},{2,4},{3,5},{4,2},{5,3},{6,0},{7,1},{8,14},{9,15},{10,... | collective-permute-start | bytes 221192 | tf_op jit(solution)/shard_map/ppermute | solution.py:171
  11.7 0.1 collective-permute-start.2
  11.8 1.9 %collective-permute-done.1 = f32[8,2304]{1,0:T(8,128)S(1)} collective-permute-done((f32[8,2304]{1,0:T(8,128)S(1)}, f32[8,2304]{1,0:T(8,128)S(1)}, u32[]{:S(2)}, u32[]{:S(2)}) %collective-permute-start.1) | collective-permute-done | bytes 73760 | tf_op jit(solution)/shard_map/ppermute | solution.py:171
  13.7 2.4 %collective-permute-done.3 = f32[8,2304]{1,0:T(8,128)S(1)} collective-permute-done((f32[8,2304]{1,0:T(8,128)S(1)}, f32[8,2304]{1,0:T(8,128)S(1)}, u32[]{:S(2)}, u32[]{:S(2)}) %collective-permute-start.3) | collective-permute-done | bytes 73760 | tf_op jit(solution)/shard_map/ppermute | solution.py:171
  16.1 0.0 collective-permute-done.2
  16.1 2.7 %collective-permute-start.4 = (f32[4,2304]{1,0:T(4,128)S(1)}, f32[4,2304]{1,0:T(4,128)S(1)}, u32[]{:S(2)}, u32[]{:S(2)}) collective-permute-start(f32[4,2304]{1,0:T(4,128)S(1)} %slice.24), channel_id=1, source_target_pairs={{0,8},{1,9},{2,10},{3,11},{4,12},{5,13},{6,14},{7,15},{8,0},{9,1},... | collective-permute-start | bytes 110600 | tf_op jit(solution)/shard_map/ppermute | solution.py:171
  18.8 2.3 %collective-permute-done.4.second_ref = f32[4,2304]{1,0:T(4,128)S(1)} collective-permute-done((f32[4,2304]{1,0:T(4,128)S(1)}, f32[4,2304]{1,0:T(4,128)S(1)}, u32[]{:S(2)}, u32[]{:S(2)}) %collective-permute-start.4) | collective-permute-done | bytes 36896 | tf_op jit(solution)/shard_map/ppermute | solution.py:171
  21.0 1.0 %expand.1 = f32[4,4096]{1,0:T(4,128)} custom-call(f32[8,2304]{1,0:T(8,128)S(1)} %fusion.1.first_ref, f32[4,2304]{1,0:T(4,128)S(1)} %collective-permute-done.4.second_ref), custom_call_target="tpu_custom_call" | custom-call | tf_op jit(solution)/shard_map/expand/pallas_call | solution.py:187
  (4 shorter events, 0.1 us)
Async XLA Ops:
  5.5 1.7 %collective-permute-start = (f32[32,2304]{1,0:T(8,128)S(1)}, f32[32,2304]{1,0:T(8,128)S(1)}, u32[]{:S(2)}, u32[]{:S(2)}) collective-permute-start(f32[32,2304]{1,0:T(8,128)S(1)} %get-tuple-element.8), channel_id=1, source_target_pairs={{0,1},{1,0},{2,3},{3,2},{4,5},{5,4},{6,7},{7,6},{8,9},{9,8},{10,11... | collective-permute-start | bytes 884744 | tf_op jit(solution)/shard_map/ppermute | solution.py:171
  7.3 6.4 %collective-permute-start.1 = (f32[8,2304]{1,0:T(8,128)S(1)}, f32[8,2304]{1,0:T(8,128)S(1)}, u32[]{:S(2)}, u32[]{:S(2)}) collective-permute-start(f32[8,2304]{1,0:T(8,128)S(1)} %get-tuple-element.9), channel_id=1, source_target_pairs={{0,2},{1,3},{2,0},{3,1},{4,6},{5,7},{6,4},{7,5},{8,10},{9,11},{10,... | collective-permute-start | bytes 221192 | tf_op jit(solution)/shard_map/ppermute | solution.py:171
  10.2 5.9 %collective-permute-start.3 = (f32[8,2304]{1,0:T(8,128)S(1)}, f32[8,2304]{1,0:T(8,128)S(1)}, u32[]{:S(2)}, u32[]{:S(2)}) collective-permute-start(f32[8,2304]{1,0:T(8,128)S(1)} %get-tuple-element.10), channel_id=1, source_target_pairs={{0,6},{1,7},{2,4},{3,5},{4,2},{5,3},{6,0},{7,1},{8,14},{9,15},{10,... | collective-permute-start | bytes 221192 | tf_op jit(solution)/shard_map/ppermute | solution.py:171
  11.7 4.4 %collective-permute-start.2 = (f32[8,2304]{1,0:T(8,128)S(1)}, f32[8,2304]{1,0:T(8,128)S(1)}, u32[]{:S(2)}, u32[]{:S(2)}) collective-permute-start(f32[8,2304]{1,0:T(8,128)S(1)} %get-tuple-element.11), channel_id=1, source_target_pairs={{0,4},{1,5},{2,6},{3,7},{4,0},{5,1},{6,2},{7,3},{8,12},{9,13},{10,... | collective-permute-start | bytes 221192 | tf_op jit(solution)/shard_map/ppermute | solution.py:171
  16.1 4.9 %collective-permute-start.4 = (f32[4,2304]{1,0:T(4,128)S(1)}, f32[4,2304]{1,0:T(4,128)S(1)}, u32[]{:S(2)}, u32[]{:S(2)}) collective-permute-start(f32[4,2304]{1,0:T(4,128)S(1)} %slice.24), channel_id=1, source_target_pairs={{0,8},{1,9},{2,10},{3,11},{4,12},{5,13},{6,14},{7,15},{8,0},{9,1},... | collective-permute-start | bytes 110600 | tf_op jit(solution)/shard_map/ppermute | solution.py:171

commit v3 on v2

--- a/solution.py
+++ b/solution.py
@@ -37,7 +37,7 @@
 
 
 def moments_kernel(axis, order, unit, step, rl_hbm, x_hbm, ql_hbm, ls_hbm, *refs):
-    *out_refs, rl_ref, x_ref, ql_ref, ls_ref, small, large = refs
+    *out_refs, rl_ref, x_ref, ql_ref, ls_ref, turned_ref, small, large = refs
     trees, rows = rl_ref.shape
     width = x_ref.shape[0]
     queries = ql_ref.shape[1]
@@ -48,18 +48,13 @@
         pltpu.make_async_copy(ql_hbm, ql_ref, small.at[0]),
         pltpu.make_async_copy(ls_hbm, ls_ref, small.at[1]),
     ]
-    pairs = []
-    for n, start in enumerate(range(0, rows, step)):
-        here = slice(start, start + step)
-        pairs.append(
-            (
-                pltpu.make_async_copy(rl_hbm.at[:, here], rl_ref.at[:, here], large.at[n, 0]),
-                pltpu.make_async_copy(x_hbm.at[:, here], x_ref.at[:, here], large.at[n, 1]),
-            )
-        )
-    for copy in copies + [copy for pair in pairs for copy in pair]:
+    copies += [
+        pltpu.make_async_copy(rl_hbm, rl_ref, large.at[0]),
+        pltpu.make_async_copy(x_hbm, x_ref, large.at[1]),
+    ]
+    for copy in copies:
         copy.start()
-    for copy in copies:
+    for copy in copies[:2]:
         copy.wait()
 
     span = max(queries, LANES)
@@ -85,11 +80,12 @@
     leaf = jnp.concatenate(leaf_parts, 0)[:queries].astype(jnp.int16)
     weight = jnp.concatenate(weight_parts, 0)[:queries].astype(jnp.int16)
 
+    for copy in copies[2:]:
+        copy.wait()
     tall = 32
-    for n, start in enumerate(range(0, rows, step)):
+    turn = turned_ref.shape[1]
+    for start in range(0, rows, step):
         here = slice(start, start + step)
-        for copy in pairs[n]:
-            copy.wait()
         row_leaf = rl_ref[:, here].astype(jnp.int16)
         parts = []
         for top in range(0, queries, tall):
@@ -104,7 +100,14 @@
         wide = x_ref[:, here].astype(jnp.float32)
         row_moments = jnp.concatenate([wide[j : j + 1] * wide[j // SUB * SUB :] for j in range(width)], 0)
         row_moments = row_moments.astype(jnp.bfloat16)
-        product = lax.dot_general(kernel_weight, row_moments, NT, preferred_element_type=jnp.float32)
+        turned_ref[...] = row_moments[:turn].T
+        product = jnp.concatenate(
+            [
+                jnp.dot(kernel_weight, turned_ref[...], preferred_element_type=jnp.float32),
+                lax.dot_general(kernel_weight, row_moments[turn:], NT, preferred_element_type=jnp.float32),
+            ],
+            1,
+        )
         top = 0
         for ref in out_refs:
             piece = product[top : top + ref.shape[0]]
@@ -148,6 +151,7 @@
 
     half = queries // 2
     step = math.gcd(local_rows, 256)
+    turn = columns // 512 * 256 + 256
     arguments = [
         pltpu.with_memory_space_constraint(a, pltpu.HBM)
         for a in (row_leaves, covariates, query_leaves, leaf_sizes)
@@ -157,7 +161,8 @@
         out_shape=[pltpu.VMEM((half, columns), jnp.float32)] * 2,
         in_specs=[pl.BlockSpec(memory_space=pltpu.HBM)] * len(arguments),
         scratch_shapes=[pltpu.VMEM(a.shape, a.dtype) for a in arguments]
-        + [pltpu.SemaphoreType.DMA((2,)), pltpu.SemaphoreType.DMA((local_rows // step, 2))],
+        + [pltpu.VMEM((step, turn), jnp.bfloat16)]
+        + [pltpu.SemaphoreType.DMA((2,))] * 2,
         compiler_params=pltpu.CompilerParams(vmem_limit_bytes=40 << 20),
         cost_estimate=pl.CostEstimate(
             flops=2 * queries * columns * local_rows,

time: 22.2 us -> 20.7 us (0.932)
  Pallas kernels: 6.42 us -> 4.9 us
    pallas_call x1, Pallas kernels: 5.45 us -> 3.93 us  [per_device(): pl.pallas_call(functools.partial(moments_kernel, axis, order, unit, step)...]
where the time goes in v3:
time: 20.7 us; the launch traced here: 20.5 us
  waiting for transfers between devices  7.77 us (38%)
  starting transfers between devices  7.71 us (37%)
  Pallas kernels  4.9 us (24%)
    ppermute x5, waiting for transfers between devices, permute(): return lax.ppermute(array, axis, [(i, i ^ shift) for i in range(count)])  7.77 us
    ppermute x5, starting transfers between devices, permute(): return lax.ppermute(array, axis, [(i, i ^ shift) for i in range(count)])  7.71 us
    pallas_call x1, Pallas kernels, per_device(): pl.pallas_call(functools.partial(moments_kernel, axis, order, unit, step)...  3.93 us
    pallas_call x1, Pallas kernels, per_device(): pl.pallas_call(functools.partial(expand_kernel, width), out_shape=jax.Sha...  0.97 us
  transfers between devices with their start and end apart: 5, of which 4 were waited for; matrix products, arithmetic and copies ran while one was open for 0% of the time, Pallas kernels for 0%

profile of v3, /device:TPU:0, one launch (start us, length us, event | category | flops | bytes accessed | tf_op | source)
XLA Modules:
  0.0 20.5 jit_solution(12494506832614777857)
XLA Ops:
  0.0 3.9 %moments.1 = (f32[32,2304]{1,0:T(8,128)S(1)}, f32[32,2304]{1,0:T(8,128)S(1)}) custom-call(s32[32,2048]{1,0:T(8,128)} %rl_hbm.1, bf16[64,2048]{1,0:T(8,128)(2,1)} %x_hbm.1, s32[32,64]{1,0:T(8,128)} %ql_hbm.1, s32[32,128]{1,0:T(8,128)} %ls_hbm.1), custom_call_target="tpu_custom_call" | custom-call | flops 603979776 | bytes 1048576 | tf_op jit(solution)/shard_map/moments/pallas_call | solution.py:159
  3.9 0.5 %collective-permute-start = (f32[32,2304]{1,0:T(8,128)S(1)}, f32[32,2304]{1,0:T(8,128)S(1)}, u32[]{:S(2)}, u32[]{:S(2)}) collective-permute-start(f32[32,2304]{1,0:T(8,128)S(1)} %get-tuple-element.8), channel_id=1, source_target_pairs={{0,1},{1,0},{2,3},{3,2},{4,5},{5,4},{6,7},{7,6},{8,9},{9,8},{10,11... | collective-permute-start | bytes 884744 | tf_op jit(solution)/shard_map/ppermute | solution.py:176
  4.5 1.2 %collective-permute-done = f32[32,2304]{1,0:T(8,128)S(1)} collective-permute-done((f32[32,2304]{1,0:T(8,128)S(1)}, f32[32,2304]{1,0:T(8,128)S(1)}, u32[]{:S(2)}, u32[]{:S(2)}) %collective-permute-start) | collective-permute-done | bytes 294944 | tf_op jit(solution)/shard_map/ppermute | solution.py:176
  5.7 3.0 %collective-permute-start.1 = (f32[8,2304]{1,0:T(8,128)S(1)}, f32[8,2304]{1,0:T(8,128)S(1)}, u32[]{:S(2)}, u32[]{:S(2)}) collective-permute-start(f32[8,2304]{1,0:T(8,128)S(1)} %get-tuple-element.9), channel_id=1, source_target_pairs={{0,2},{1,3},{2,0},{3,1},{4,6},{5,7},{6,4},{7,5},{8,10},{9,11},{10,... | collective-permute-start | bytes 221192 | tf_op jit(solution)/shard_map/ppermute | solution.py:176
  8.7 1.5 %collective-permute-start.3 = (f32[8,2304]{1,0:T(8,128)S(1)}, f32[8,2304]{1,0:T(8,128)S(1)}, u32[]{:S(2)}, u32[]{:S(2)}) collective-permute-start(f32[8,2304]{1,0:T(8,128)S(1)} %get-tuple-element.10), channel_id=1, source_target_pairs={{0,6},{1,7},{2,4},{3,5},{4,2},{5,3},{6,0},{7,1},{8,14},{9,15},{10,... | collective-permute-start | bytes 221192 | tf_op jit(solution)/shard_map/ppermute | solution.py:176
  10.2 0.1 collective-permute-start.2
  10.3 1.9 %collective-permute-done.1 = f32[8,2304]{1,0:T(8,128)S(1)} collective-permute-done((f32[8,2304]{1,0:T(8,128)S(1)}, f32[8,2304]{1,0:T(8,128)S(1)}, u32[]{:S(2)}, u32[]{:S(2)}) %collective-permute-start.1) | collective-permute-done | bytes 73760 | tf_op jit(solution)/shard_map/ppermute | solution.py:176
  12.2 2.4 %collective-permute-done.3 = f32[8,2304]{1,0:T(8,128)S(1)} collective-permute-done((f32[8,2304]{1,0:T(8,128)S(1)}, f32[8,2304]{1,0:T(8,128)S(1)}, u32[]{:S(2)}, u32[]{:S(2)}) %collective-permute-start.3) | collective-permute-done | bytes 73760 | tf_op jit(solution)/shard_map/ppermute | solution.py:176
  14.5 0.0 collective-permute-done.2
  14.6 2.7 %collective-permute-start.4 = (f32[4,2304]{1,0:T(4,128)S(1)}, f32[4,2304]{1,0:T(4,128)S(1)}, u32[]{:S(2)}, u32[]{:S(2)}) collective-permute-start(f32[4,2304]{1,0:T(4,128)S(1)} %slice.24), channel_id=1, source_target_pairs={{0,8},{1,9},{2,10},{3,11},{4,12},{5,13},{6,14},{7,15},{8,0},{9,1},... | collective-permute-start | bytes 110600 | tf_op jit(solution)/shard_map/ppermute | solution.py:176
  17.3 2.3 %collective-permute-done.4.second_ref = f32[4,2304]{1,0:T(4,128)S(1)} collective-permute-done((f32[4,2304]{1,0:T(4,128)S(1)}, f32[4,2304]{1,0:T(4,128)S(1)}, u32[]{:S(2)}, u32[]{:S(2)}) %collective-permute-start.4) | collective-permute-done | bytes 36896 | tf_op jit(solution)/shard_map/ppermute | solution.py:176
  19.5 1.0 %expand.1 = f32[4,4096]{1,0:T(4,128)} custom-call(f32[8,2304]{1,0:T(8,128)S(1)} %fusion.1.first_ref, f32[4,2304]{1,0:T(4,128)S(1)} %collective-permute-done.4.second_ref), custom_call_target="tpu_custom_call" | custom-call | tf_op jit(solution)/shard_map/expand/pallas_call | solution.py:192
  (4 shorter events, 0.1 us)
Async XLA Ops:
  3.9 1.7 %collective-permute-start = (f32[32,2304]{1,0:T(8,128)S(1)}, f32[32,2304]{1,0:T(8,128)S(1)}, u32[]{:S(2)}, u32[]{:S(2)}) collective-permute-start(f32[32,2304]{1,0:T(8,128)S(1)} %get-tuple-element.8), channel_id=1, source_target_pairs={{0,1},{1,0},{2,3},{3,2},{4,5},{5,4},{6,7},{7,6},{8,9},{9,8},{10,11... | collective-permute-start | bytes 884744 | tf_op jit(solution)/shard_map/ppermute | solution.py:176
  5.7 6.4 %collective-permute-start.1 = (f32[8,2304]{1,0:T(8,128)S(1)}, f32[8,2304]{1,0:T(8,128)S(1)}, u32[]{:S(2)}, u32[]{:S(2)}) collective-permute-start(f32[8,2304]{1,0:T(8,128)S(1)} %get-tuple-element.9), channel_id=1, source_target_pairs={{0,2},{1,3},{2,0},{3,1},{4,6},{5,7},{6,4},{7,5},{8,10},{9,11},{10,... | collective-permute-start | bytes 221192 | tf_op jit(solution)/shard_map/ppermute | solution.py:176
  8.7 5.9 %collective-permute-start.3 = (f32[8,2304]{1,0:T(8,128)S(1)}, f32[8,2304]{1,0:T(8,128)S(1)}, u32[]{:S(2)}, u32[]{:S(2)}) collective-permute-start(f32[8,2304]{1,0:T(8,128)S(1)} %get-tuple-element.10), channel_id=1, source_target_pairs={{0,6},{1,7},{2,4},{3,5},{4,2},{5,3},{6,0},{7,1},{8,14},{9,15},{10,... | collective-permute-start | bytes 221192 | tf_op jit(solution)/shard_map/ppermute | solution.py:176
  10.2 4.4 %collective-permute-start.2 = (f32[8,2304]{1,0:T(8,128)S(1)}, f32[8,2304]{1,0:T(8,128)S(1)}, u32[]{:S(2)}, u32[]{:S(2)}) collective-permute-start(f32[8,2304]{1,0:T(8,128)S(1)} %get-tuple-element.11), channel_id=1, source_target_pairs={{0,4},{1,5},{2,6},{3,7},{4,0},{5,1},{6,2},{7,3},{8,12},{9,13},{10,... | collective-permute-start | bytes 221192 | tf_op jit(solution)/shard_map/ppermute | solution.py:176
  14.6 4.9 %collective-permute-start.4 = (f32[4,2304]{1,0:T(4,128)S(1)}, f32[4,2304]{1,0:T(4,128)S(1)}, u32[]{:S(2)}, u32[]{:S(2)}) collective-permute-start(f32[4,2304]{1,0:T(4,128)S(1)} %slice.24), channel_id=1, source_target_pairs={{0,8},{1,9},{2,10},{3,11},{4,12},{5,13},{6,14},{7,15},{8,0},{9,1},... | collective-permute-start | bytes 110600 | tf_op jit(solution)/shard_map/ppermute | solution.py:176

commit v4 on v3

--- a/solution.py
+++ b/solution.py
@@ -1,5 +1,6 @@
 import functools
 import math
+import operator
 
 import jax
 import jax.numpy as jnp
@@ -25,14 +26,21 @@
 def stages(count):
     bits = [1 << i for i in range(count.bit_length() - 1)]
     rest = bits[1:]
-    return [bits[:1]] * (count > 1) + [rest[i : i + 2] for i in range(0, len(rest), 2)]
+    found = [bits[:1]] * (count > 1)
+    for i in range(0, len(rest), 2):
+        pair = rest[i : i + 2]
+        found.append([shift ^ 1 for shift in pair])
+    return found
+
+
+def combine(group, s):
+    return functools.reduce(operator.xor, (shift for i, shift in enumerate(group) if (s >> i) & 1), 0)
 
 
 def block_order(count):
     order = [0]
     for group in reversed(stages(count)):
-        shifts = [sum(b for i, b in enumerate(group) if (s >> i) & 1) for s in range(1 << len(group))]
-        order = [s | p for s in shifts for p in order]
+        order = [combine(group, s) ^ p for s in range(1 << len(group)) for p in order]
     return order
 
 
@@ -61,7 +69,7 @@
     place = lax.broadcasted_iota(jnp.int32, (trees, span), 1)
     block = jnp.zeros((trees, span), jnp.int32)
     for i in range(len(order).bit_length() - 1):
-        block += ((place // share >> i) & 1) * order[1 << i]
+        block ^= ((place // share >> i) & 1) * order[1 << i]
     source = ((block ^ me) * share + place % share) % queries
     leaves = ql_ref[...]
     if queries < span:
@@ -182,8 +190,7 @@
         size = total.shape[0] // blocks
         arrived = []
         for s in range(1, blocks):
-            shift = sum(b for i, b in enumerate(group) if (s >> i) & 1)
-            arrived.append(permute(total[s * size : (s + 1) * size], shift))
+            arrived.append(permute(total[s * size : (s + 1) * size], combine(group, s)))
         first = total
         for extra in arrived[:-1]:
             first = first[:size] + extra

time: 20.7 us -> 20 us (0.966)
  starting transfers between devices: 7.71 us -> 7.18 us
  waiting for transfers between devices: 7.77 us -> 7.53 us
    ppermute x5, starting transfers between devices: 7.71 us -> 7.18 us  [permute(): return lax.ppermute(array, axis, [(i, i ^ shift) for i in range(count)])]
    ppermute x5, waiting for transfers between devices: 7.77 us -> 7.53 us  [permute(): return lax.ppermute(array, axis, [(i, i ^ shift) for i in range(count)])]
  transfers between devices with their start and end apart: 5 -> 5, of which waited for: 4 -> 5; matrix products, arithmetic and copies ran while one was open for 0% -> 0% of each run, Pallas kernels for 0% -> 0%
where the time goes in v4:
time: 20 us; the launch traced here: 19.7 us
  waiting for transfers between devices  7.53 us (38%)
  starting transfers between devices  7.18 us (36%)
  Pallas kernels  4.9 us (25%)
    ppermute x5, waiting for transfers between devices, permute(): return lax.ppermute(array, axis, [(i, i ^ shift) for i in range(count)])  7.53 us
    ppermute x5, starting transfers between devices, permute(): return lax.ppermute(array, axis, [(i, i ^ shift) for i in range(count)])  7.18 us
    pallas_call x1, Pallas kernels, per_device(): pl.pallas_call(functools.partial(moments_kernel, axis, order, unit, step)...  3.93 us
    pallas_call x1, Pallas kernels, per_device(): pl.pallas_call(functools.partial(expand_kernel, width), out_shape=jax.Sha...  0.97 us
  transfers between devices with their start and end apart: 5, of which 5 were waited for; matrix products, arithmetic and copies ran while one was open for 0% of the time, Pallas kernels for 0%

profile of v4, /device:TPU:0, one launch (start us, length us, event | category | flops | bytes accessed | tf_op | source)
XLA Modules:
  0.0 19.7 jit_solution(14627941659808420451)
XLA Ops:
  0.0 3.9 %moments.1 = (f32[32,2304]{1,0:T(8,128)S(1)}, f32[32,2304]{1,0:T(8,128)S(1)}) custom-call(s32[32,2048]{1,0:T(8,128)} %rl_hbm.1, bf16[64,2048]{1,0:T(8,128)(2,1)} %x_hbm.1, s32[32,64]{1,0:T(8,128)} %ql_hbm.1, s32[32,128]{1,0:T(8,128)} %ls_hbm.1), custom_call_target="tpu_custom_call" | custom-call | flops 603979776 | bytes 1048576 | tf_op jit(solution)/shard_map/moments/pallas_call | solution.py:167
  3.9 0.5 %collective-permute-start = (f32[32,2304]{1,0:T(8,128)S(1)}, f32[32,2304]{1,0:T(8,128)S(1)}, u32[]{:S(2)}, u32[]{:S(2)}) collective-permute-start(f32[32,2304]{1,0:T(8,128)S(1)} %get-tuple-element.8), channel_id=1, source_target_pairs={{0,1},{1,0},{2,3},{3,2},{4,5},{5,4},{6,7},{7,6},{8,9},{9,8},{10,11... | collective-permute-start | bytes 884744 | tf_op jit(solution)/shard_map/ppermute | solution.py:184
  4.5 1.2 %collective-permute-done = f32[32,2304]{1,0:T(8,128)S(1)} collective-permute-done((f32[32,2304]{1,0:T(8,128)S(1)}, f32[32,2304]{1,0:T(8,128)S(1)}, u32[]{:S(2)}, u32[]{:S(2)}) %collective-permute-start) | collective-permute-done | bytes 294944 | tf_op jit(solution)/shard_map/ppermute | solution.py:184
  5.7 2.7 %collective-permute-start.1 = (f32[8,2304]{1,0:T(8,128)S(1)}, f32[8,2304]{1,0:T(8,128)S(1)}, u32[]{:S(2)}, u32[]{:S(2)}) collective-permute-start(f32[8,2304]{1,0:T(8,128)S(1)} %get-tuple-element.9), channel_id=1, source_target_pairs={{0,3},{1,2},{2,1},{3,0},{4,7},{5,6},{6,5},{7,4},{8,11},{9,10},{10,... | collective-permute-start | bytes 221192 | tf_op jit(solution)/shard_map/ppermute | solution.py:184
  8.4 1.5 %collective-permute-start.3 = (f32[8,2304]{1,0:T(8,128)S(1)}, f32[8,2304]{1,0:T(8,128)S(1)}, u32[]{:S(2)}, u32[]{:S(2)}) collective-permute-start(f32[8,2304]{1,0:T(8,128)S(1)} %get-tuple-element.10), channel_id=1, source_target_pairs={{0,6},{1,7},{2,4},{3,5},{4,2},{5,3},{6,0},{7,1},{8,14},{9,15},{10,... | collective-permute-start | bytes 221192 | tf_op jit(solution)/shard_map/ppermute | solution.py:184
  10.0 0.0 collective-permute-start.2
  10.0 2.4 %collective-permute-done.1 = f32[8,2304]{1,0:T(8,128)S(1)} collective-permute-done((f32[8,2304]{1,0:T(8,128)S(1)}, f32[8,2304]{1,0:T(8,128)S(1)}, u32[]{:S(2)}, u32[]{:S(2)}) %collective-permute-start.1) | collective-permute-done | bytes 73760 | tf_op jit(solution)/shard_map/ppermute | solution.py:184
  12.4 1.5 %collective-permute-done.3 = f32[8,2304]{1,0:T(8,128)S(1)} collective-permute-done((f32[8,2304]{1,0:T(8,128)S(1)}, f32[8,2304]{1,0:T(8,128)S(1)}, u32[]{:S(2)}, u32[]{:S(2)}) %collective-permute-start.3) | collective-permute-done | bytes 73760 | tf_op jit(solution)/shard_map/ppermute | solution.py:184
  13.9 0.4 %collective-permute-done.2 = f32[8,2304]{1,0:T(8,128)S(1)} collective-permute-done((f32[8,2304]{1,0:T(8,128)S(1)}, f32[8,2304]{1,0:T(8,128)S(1)}, u32[]{:S(2)}, u32[]{:S(2)}) %collective-permute-start.2) | collective-permute-done | bytes 73760 | tf_op jit(solution)/shard_map/ppermute | solution.py:184
  14.3 2.4 %collective-permute-start.4 = (f32[4,2304]{1,0:T(4,128)S(1)}, f32[4,2304]{1,0:T(4,128)S(1)}, u32[]{:S(2)}, u32[]{:S(2)}) collective-permute-start(f32[4,2304]{1,0:T(4,128)S(1)} %slice.24), channel_id=1, source_target_pairs={{0,9},{1,8},{2,11},{3,10},{4,13},{5,12},{6,15},{7,14},{8,1},{9,0},... | collective-permute-start | bytes 110600 | tf_op jit(solution)/shard_map/ppermute | solution.py:184
  16.7 2.0 %collective-permute-done.4.second_ref = f32[4,2304]{1,0:T(4,128)S(1)} collective-permute-done((f32[4,2304]{1,0:T(4,128)S(1)}, f32[4,2304]{1,0:T(4,128)S(1)}, u32[]{:S(2)}, u32[]{:S(2)}) %collective-permute-start.4) | collective-permute-done | bytes 36896 | tf_op jit(solution)/shard_map/ppermute | solution.py:184
  18.8 1.0 %expand.1 = f32[4,4096]{1,0:T(4,128)} custom-call(f32[8,2304]{1,0:T(8,128)S(1)} %fusion.1.first_ref, f32[4,2304]{1,0:T(4,128)S(1)} %collective-permute-done.4.second_ref), custom_call_target="tpu_custom_call" | custom-call | tf_op jit(solution)/shard_map/expand/pallas_call | solution.py:199
  (4 shorter events, 0.1 us)
Async XLA Ops:
  3.9 1.7 %collective-permute-start = (f32[32,2304]{1,0:T(8,128)S(1)}, f32[32,2304]{1,0:T(8,128)S(1)}, u32[]{:S(2)}, u32[]{:S(2)}) collective-permute-start(f32[32,2304]{1,0:T(8,128)S(1)} %get-tuple-element.8), channel_id=1, source_target_pairs={{0,1},{1,0},{2,3},{3,2},{4,5},{5,4},{6,7},{7,6},{8,9},{9,8},{10,11... | collective-permute-start | bytes 884744 | tf_op jit(solution)/shard_map/ppermute | solution.py:184
  5.7 6.7 %collective-permute-start.1 = (f32[8,2304]{1,0:T(8,128)S(1)}, f32[8,2304]{1,0:T(8,128)S(1)}, u32[]{:S(2)}, u32[]{:S(2)}) collective-permute-start(f32[8,2304]{1,0:T(8,128)S(1)} %get-tuple-element.9), channel_id=1, source_target_pairs={{0,3},{1,2},{2,1},{3,0},{4,7},{5,6},{6,5},{7,4},{8,11},{9,10},{10,... | collective-permute-start | bytes 221192 | tf_op jit(solution)/shard_map/ppermute | solution.py:184
  8.4 5.4 %collective-permute-start.3 = (f32[8,2304]{1,0:T(8,128)S(1)}, f32[8,2304]{1,0:T(8,128)S(1)}, u32[]{:S(2)}, u32[]{:S(2)}) collective-permute-start(f32[8,2304]{1,0:T(8,128)S(1)} %get-tuple-element.10), channel_id=1, source_target_pairs={{0,6},{1,7},{2,4},{3,5},{4,2},{5,3},{6,0},{7,1},{8,14},{9,15},{10,... | collective-permute-start | bytes 221192 | tf_op jit(solution)/shard_map/ppermute | solution.py:184
  10.0 4.3 %collective-permute-start.2 = (f32[8,2304]{1,0:T(8,128)S(1)}, f32[8,2304]{1,0:T(8,128)S(1)}, u32[]{:S(2)}, u32[]{:S(2)}) collective-permute-start(f32[8,2304]{1,0:T(8,128)S(1)} %get-tuple-element.11), channel_id=1, source_target_pairs={{0,5},{1,4},{2,7},{3,6},{4,1},{5,0},{6,3},{7,2},{8,13},{9,12},{10,... | collective-permute-start | bytes 221192 | tf_op jit(solution)/shard_map/ppermute | solution.py:184
  14.3 4.4 %collective-permute-start.4 = (f32[4,2304]{1,0:T(4,128)S(1)}, f32[4,2304]{1,0:T(4,128)S(1)}, u32[]{:S(2)}, u32[]{:S(2)}) collective-permute-start(f32[4,2304]{1,0:T(4,128)S(1)} %slice.24), channel_id=1, source_target_pairs={{0,9},{1,8},{2,11},{3,10},{4,13},{5,12},{6,15},{7,14},{8,1},{9,0},... | collective-permute-start | bytes 110600 | tf_op jit(solution)/shard_map/ppermute | solution.py:184

commit v5 on v4

--- a/solution.py
+++ b/solution.py
@@ -15,12 +15,19 @@
 
 
 def segments(width):
-    found, offset = [], 0
+    blocks = width // SUB
+    found = []
     for j in range(width):
-        first = j // SUB * SUB
-        found.append((offset, first))
-        offset += width - first
-    return found, offset
+        block, row = divmod(j, SUB)
+        first = block * SUB
+        if 2 * block < blocks:
+            found.append((j * width + first, first))
+        elif 2 * block == blocks:
+            window = first + row % (SUB // 2)
+            found.append((window * width + (first if 2 * row < SUB else 0), first))
+        else:
+            found.append((((blocks - block) * SUB + row) * width, first))
+    return found, (width + SUB) * width // 2
 
 
 def stages(count):
@@ -90,8 +97,9 @@
 
     for copy in copies[2:]:
         copy.wait()
-    tall = 32
+    tall = 16
     turn = turned_ref.shape[1]
+    placed = sorted((offset, first, j) for j, (offset, first) in enumerate(segments(width)[0]))
     for start in range(0, rows, step):
         here = slice(start, start + step)
         row_leaf = rl_ref[:, here].astype(jnp.int16)
@@ -106,7 +114,7 @@
             parts.append((total.astype(jnp.float32) * (1.0 / unit)).astype(jnp.bfloat16))
         kernel_weight = jnp.concatenate(parts, 0)
         wide = x_ref[:, here].astype(jnp.float32)
-        row_moments = jnp.concatenate([wide[j : j + 1] * wide[j // SUB * SUB :] for j in range(width)], 0)
+        row_moments = jnp.concatenate([wide[j : j + 1] * wide[first:] for _, first, j in placed], 0)
         row_moments = row_moments.astype(jnp.bfloat16)
         turned_ref[...] = row_moments[:turn].T
         product = jnp.concatenate(
@@ -138,9 +146,10 @@
         square = held[pl.ds(q, width, stride=tall), :][:, :width]
         whole = jnp.where(upper, square, square.T)
         full[pl.ds(q, width, stride=tall), :] = jnp.concatenate([whole] * (LANES // width), axis=1)
-    for j in range(width):
-        lane = j * width % LANES
-        out_ref[:, j * width : (j + 1) * width] = full[j * tall : j * tall + share, lane : lane + width]
+    copies = LANES // width
+    for j in range(0, width, copies):
+        rows = [full[(j + h) * tall : (j + h) * tall + share, h * width : (h + 1) * width] for h in range(copies)]
+        out_ref[:, j * width : (j + copies) * width] = jnp.concatenate(rows, 1)
 
 
 def per_device(row_leaves, covariates, query_leaves, leaf_sizes):

time: 20 us -> 19.9 us (level)
  no operation moved by 1% of the time
where the time goes in v5:
time: 19.9 us; the launch traced here: 19.6 us
  waiting for transfers between devices  7.53 us (38%)
  starting transfers between devices  7.17 us (36%)
  Pallas kernels  4.81 us (24%)
    ppermute x5, waiting for transfers between devices, permute(): return lax.ppermute(array, axis, [(i, i ^ shift) for i in range(count)])  7.53 us
    ppermute x5, starting transfers between devices, permute(): return lax.ppermute(array, axis, [(i, i ^ shift) for i in range(count)])  7.17 us
    pallas_call x1, Pallas kernels, per_device(): pl.pallas_call(functools.partial(moments_kernel, axis, order, unit, step)...  3.86 us
    pallas_call x1, Pallas kernels, per_device(): pl.pallas_call(functools.partial(expand_kernel, width), out_shape=jax.Sha...  0.95 us
  transfers between devices with their start and end apart: 5, of which 5 were waited for; matrix products, arithmetic and copies ran while one was open for 0% of the time, Pallas kernels for 0%

profile of v5, /device:TPU:0, one launch (start us, length us, event | category | flops | bytes accessed | tf_op | source)
XLA Modules:
  0.0 19.6 jit_solution(8889625880332406756)
XLA Ops:
  0.0 3.9 %moments.1 = (f32[32,2304]{1,0:T(8,128)S(1)}, f32[32,2304]{1,0:T(8,128)S(1)}) custom-call(s32[32,2048]{1,0:T(8,128)} %rl_hbm.1, bf16[64,2048]{1,0:T(8,128)(2,1)} %x_hbm.1, s32[32,64]{1,0:T(8,128)} %ql_hbm.1, s32[32,128]{1,0:T(8,128)} %ls_hbm.1), custom_call_target="tpu_custom_call" | custom-call | flops 603979776 | bytes 1048576 | tf_op jit(solution)/shard_map/moments/pallas_call | solution.py:176
  3.9 0.5 %collective-permute-start = (f32[32,2304]{1,0:T(8,128)S(1)}, f32[32,2304]{1,0:T(8,128)S(1)}, u32[]{:S(2)}, u32[]{:S(2)}) collective-permute-start(f32[32,2304]{1,0:T(8,128)S(1)} %get-tuple-element.8), channel_id=1, source_target_pairs={{0,1},{1,0},{2,3},{3,2},{4,5},{5,4},{6,7},{7,6},{8,9},{9,8},{10,11... | collective-permute-start | bytes 884744 | tf_op jit(solution)/shard_map/ppermute | solution.py:193
  4.4 1.2 %collective-permute-done = f32[32,2304]{1,0:T(8,128)S(1)} collective-permute-done((f32[32,2304]{1,0:T(8,128)S(1)}, f32[32,2304]{1,0:T(8,128)S(1)}, u32[]{:S(2)}, u32[]{:S(2)}) %collective-permute-start) | collective-permute-done | bytes 294944 | tf_op jit(solution)/shard_map/ppermute | solution.py:193
  5.7 2.7 %collective-permute-start.1 = (f32[8,2304]{1,0:T(8,128)S(1)}, f32[8,2304]{1,0:T(8,128)S(1)}, u32[]{:S(2)}, u32[]{:S(2)}) collective-permute-start(f32[8,2304]{1,0:T(8,128)S(1)} %get-tuple-element.9), channel_id=1, source_target_pairs={{0,3},{1,2},{2,1},{3,0},{4,7},{5,6},{6,5},{7,4},{8,11},{9,10},{10,... | collective-permute-start | bytes 221192 | tf_op jit(solution)/shard_map/ppermute | solution.py:193
  8.4 1.5 %collective-permute-start.3 = (f32[8,2304]{1,0:T(8,128)S(1)}, f32[8,2304]{1,0:T(8,128)S(1)}, u32[]{:S(2)}, u32[]{:S(2)}) collective-permute-start(f32[8,2304]{1,0:T(8,128)S(1)} %get-tuple-element.10), channel_id=1, source_target_pairs={{0,6},{1,7},{2,4},{3,5},{4,2},{5,3},{6,0},{7,1},{8,14},{9,15},{10,... | collective-permute-start | bytes 221192 | tf_op jit(solution)/shard_map/ppermute | solution.py:193
  9.9 0.0 collective-permute-start.2
  9.9 2.4 %collective-permute-done.1 = f32[8,2304]{1,0:T(8,128)S(1)} collective-permute-done((f32[8,2304]{1,0:T(8,128)S(1)}, f32[8,2304]{1,0:T(8,128)S(1)}, u32[]{:S(2)}, u32[]{:S(2)}) %collective-permute-start.1) | collective-permute-done | bytes 73760 | tf_op jit(solution)/shard_map/ppermute | solution.py:193
  12.3 1.5 %collective-permute-done.3 = f32[8,2304]{1,0:T(8,128)S(1)} collective-permute-done((f32[8,2304]{1,0:T(8,128)S(1)}, f32[8,2304]{1,0:T(8,128)S(1)}, u32[]{:S(2)}, u32[]{:S(2)}) %collective-permute-start.3) | collective-permute-done | bytes 73760 | tf_op jit(solution)/shard_map/ppermute | solution.py:193
  13.8 0.4 %collective-permute-done.2 = f32[8,2304]{1,0:T(8,128)S(1)} collective-permute-done((f32[8,2304]{1,0:T(8,128)S(1)}, f32[8,2304]{1,0:T(8,128)S(1)}, u32[]{:S(2)}, u32[]{:S(2)}) %collective-permute-start.2) | collective-permute-done | bytes 73760 | tf_op jit(solution)/shard_map/ppermute | solution.py:193
  14.2 2.4 %collective-permute-start.4 = (f32[4,2304]{1,0:T(4,128)S(1)}, f32[4,2304]{1,0:T(4,128)S(1)}, u32[]{:S(2)}, u32[]{:S(2)}) collective-permute-start(f32[4,2304]{1,0:T(4,128)S(1)} %slice.24), channel_id=1, source_target_pairs={{0,9},{1,8},{2,11},{3,10},{4,13},{5,12},{6,15},{7,14},{8,1},{9,0},... | collective-permute-start | bytes 110600 | tf_op jit(solution)/shard_map/ppermute | solution.py:193
  16.6 2.0 %collective-permute-done.4.second_ref = f32[4,2304]{1,0:T(4,128)S(1)} collective-permute-done((f32[4,2304]{1,0:T(4,128)S(1)}, f32[4,2304]{1,0:T(4,128)S(1)}, u32[]{:S(2)}, u32[]{:S(2)}) %collective-permute-start.4) | collective-permute-done | bytes 36896 | tf_op jit(solution)/shard_map/ppermute | solution.py:193
  18.7 0.9 %expand.1 = f32[4,4096]{1,0:T(4,128)} custom-call(f32[8,2304]{1,0:T(8,128)S(1)} %fusion.1.first_ref, f32[4,2304]{1,0:T(4,128)S(1)} %collective-permute-done.4.second_ref), custom_call_target="tpu_custom_call" | custom-call | tf_op jit(solution)/shard_map/expand/pallas_call | solution.py:208
  (4 shorter events, 0.1 us)
Async XLA Ops:
  3.9 1.7 %collective-permute-start = (f32[32,2304]{1,0:T(8,128)S(1)}, f32[32,2304]{1,0:T(8,128)S(1)}, u32[]{:S(2)}, u32[]{:S(2)}) collective-permute-start(f32[32,2304]{1,0:T(8,128)S(1)} %get-tuple-element.8), channel_id=1, source_target_pairs={{0,1},{1,0},{2,3},{3,2},{4,5},{5,4},{6,7},{7,6},{8,9},{9,8},{10,11... | collective-permute-start | bytes 884744 | tf_op jit(solution)/shard_map/ppermute | solution.py:193
  5.7 6.7 %collective-permute-start.1 = (f32[8,2304]{1,0:T(8,128)S(1)}, f32[8,2304]{1,0:T(8,128)S(1)}, u32[]{:S(2)}, u32[]{:S(2)}) collective-permute-start(f32[8,2304]{1,0:T(8,128)S(1)} %get-tuple-element.9), channel_id=1, source_target_pairs={{0,3},{1,2},{2,1},{3,0},{4,7},{5,6},{6,5},{7,4},{8,11},{9,10},{10,... | collective-permute-start | bytes 221192 | tf_op jit(solution)/shard_map/ppermute | solution.py:193
  8.4 5.4 %collective-permute-start.3 = (f32[8,2304]{1,0:T(8,128)S(1)}, f32[8,2304]{1,0:T(8,128)S(1)}, u32[]{:S(2)}, u32[]{:S(2)}) collective-permute-start(f32[8,2304]{1,0:T(8,128)S(1)} %get-tuple-element.10), channel_id=1, source_target_pairs={{0,6},{1,7},{2,4},{3,5},{4,2},{5,3},{6,0},{7,1},{8,14},{9,15},{10,... | collective-permute-start | bytes 221192 | tf_op jit(solution)/shard_map/ppermute | solution.py:193
  9.9 4.3 %collective-permute-start.2 = (f32[8,2304]{1,0:T(8,128)S(1)}, f32[8,2304]{1,0:T(8,128)S(1)}, u32[]{:S(2)}, u32[]{:S(2)}) collective-permute-start(f32[8,2304]{1,0:T(8,128)S(1)} %get-tuple-element.11), channel_id=1, source_target_pairs={{0,5},{1,4},{2,7},{3,6},{4,1},{5,0},{6,3},{7,2},{8,13},{9,12},{10,... | collective-permute-start | bytes 221192 | tf_op jit(solution)/shard_map/ppermute | solution.py:193
  14.2 4.4 %collective-permute-start.4 = (f32[4,2304]{1,0:T(4,128)S(1)}, f32[4,2304]{1,0:T(4,128)S(1)}, u32[]{:S(2)}, u32[]{:S(2)}) collective-permute-start(f32[4,2304]{1,0:T(4,128)S(1)} %slice.24), channel_id=1, source_target_pairs={{0,9},{1,8},{2,11},{3,10},{4,13},{5,12},{6,15},{7,14},{8,1},{9,0},... | collective-permute-start | bytes 110600 | tf_op jit(solution)/shard_map/ppermute | solution.py:193

commit v6 on v5

--- a/solution.py
+++ b/solution.py
@@ -52,7 +52,8 @@
 
 
 def moments_kernel(axis, order, unit, step, rl_hbm, x_hbm, ql_hbm, ls_hbm, *refs):
-    *out_refs, rl_ref, x_ref, ql_ref, ls_ref, turned_ref, small, large = refs
+    *out_refs, rl_ref, x_ref, ql_ref, ls_ref, t0, t1, s0, s1, small, large = refs
+    turned_refs, straight_refs = (t0, t1), (s0, s1)
     trees, rows = rl_ref.shape
     width = x_ref.shape[0]
     queries = ql_ref.shape[1]
@@ -98,7 +99,24 @@
     for copy in copies[2:]:
         copy.wait()
     tall = 16
-    turn = turned_ref.shape[1]
+    turn = t0.shape[1]
+    waiting = []
+
+    def add(start, kernel_weight):
+        slot = start // step % 2
+        product = jnp.concatenate(
+            [
+                jnp.dot(kernel_weight, turned_refs[slot][...], preferred_element_type=jnp.float32),
+                lax.dot_general(kernel_weight, straight_refs[slot][...], NT, preferred_element_type=jnp.float32),
+            ],
+            1,
+        )
+        top = 0
+        for ref in out_refs:
+            piece = product[top : top + ref.shape[0]]
+            ref[...] = piece if start == 0 else ref[...] + piece
+            top += ref.shape[0]
+
     placed = sorted((offset, first, j) for j, (offset, first) in enumerate(segments(width)[0]))
     for start in range(0, rows, step):
         here = slice(start, start + step)
@@ -116,19 +134,12 @@
         wide = x_ref[:, here].astype(jnp.float32)
         row_moments = jnp.concatenate([wide[j : j + 1] * wide[first:] for _, first, j in placed], 0)
         row_moments = row_moments.astype(jnp.bfloat16)
-        turned_ref[...] = row_moments[:turn].T
-        product = jnp.concatenate(
-            [
-                jnp.dot(kernel_weight, turned_ref[...], preferred_element_type=jnp.float32),
-                lax.dot_general(kernel_weight, row_moments[turn:], NT, preferred_element_type=jnp.float32),
-            ],
-            1,
-        )
-        top = 0
-        for ref in out_refs:
-            piece = product[top : top + ref.shape[0]]
-            ref[...] = piece if start == 0 else ref[...] + piece
-            top += ref.shape[0]
+        turned_refs[start // step % 2][...] = row_moments[:turn].T
+        straight_refs[start // step % 2][...] = row_moments[turn:]
+        waiting.append((start, kernel_weight))
+        if len(waiting) > 1:
+            add(*waiting.pop(0))
+    add(*waiting.pop(0))
 
 
 def expand_kernel(width, first_ref, second_ref, out_ref, held, full):
@@ -178,7 +189,8 @@
         out_shape=[pltpu.VMEM((half, columns), jnp.float32)] * 2,
         in_specs=[pl.BlockSpec(memory_space=pltpu.HBM)] * len(arguments),
         scratch_shapes=[pltpu.VMEM(a.shape, a.dtype) for a in arguments]
-        + [pltpu.VMEM((step, turn), jnp.bfloat16)]
+        + [pltpu.VMEM((step, turn), jnp.bfloat16)] * 2
+        + [pltpu.VMEM((columns - turn, step), jnp.bfloat16)] * 2
         + [pltpu.SemaphoreType.DMA((2,))] * 2,
         compiler_params=pltpu.CompilerParams(vmem_limit_bytes=40 << 20),
         cost_estimate=pl.CostEstimate(

time: 19.9 us -> 19.9 us (level)
  no operation moved by 1% of the time
where the time goes in v6:
time: 19.9 us; the launch traced here: 19.6 us
  waiting for transfers between devices  7.53 us (38%)
  starting transfers between devices  7.17 us (36%)
  Pallas kernels  4.81 us (24%)
    ppermute x5, waiting for transfers between devices, permute(): return lax.ppermute(array, axis, [(i, i ^ shift) for i in range(count)])  7.53 us
    ppermute x5, starting transfers between devices, permute(): return lax.ppermute(array, axis, [(i, i ^ shift) for i in range(count)])  7.17 us
    pallas_call x1, Pallas kernels, per_device(): pl.pallas_call(functools.partial(moments_kernel, axis, order, unit, step)...  3.86 us
    pallas_call x1, Pallas kernels, per_device(): pl.pallas_call(functools.partial(expand_kernel, width), out_shape=jax.Sha...  0.95 us
  transfers between devices with their start and end apart: 5, of which 5 were waited for; matrix products, arithmetic and copies ran while one was open for 0% of the time, Pallas kernels for 0%

profile of v6, /device:TPU:0, one launch (start us, length us, event | category | flops | bytes accessed | tf_op | source)
XLA Modules:
  0.0 19.6 jit_solution(8889625880332406756)
XLA Ops:
  0.0 3.9 %moments.1 = (f32[32,2304]{1,0:T(8,128)S(1)}, f32[32,2304]{1,0:T(8,128)S(1)}) custom-call(s32[32,2048]{1,0:T(8,128)} %rl_hbm.1, bf16[64,2048]{1,0:T(8,128)(2,1)} %x_hbm.1, s32[32,64]{1,0:T(8,128)} %ql_hbm.1, s32[32,128]{1,0:T(8,128)} %ls_hbm.1), custom_call_target="tpu_custom_call" | custom-call | flops 603979776 | bytes 1048576 | tf_op jit(solution)/shard_map/moments/pallas_call | solution.py:187
  3.9 0.5 %collective-permute-start = (f32[32,2304]{1,0:T(8,128)S(1)}, f32[32,2304]{1,0:T(8,128)S(1)}, u32[]{:S(2)}, u32[]{:S(2)}) collective-permute-start(f32[32,2304]{1,0:T(8,128)S(1)} %get-tuple-element.8), channel_id=1, source_target_pairs={{0,1},{1,0},{2,3},{3,2},{4,5},{5,4},{6,7},{7,6},{8,9},{9,8},{10,11... | collective-permute-start | bytes 884744 | tf_op jit(solution)/shard_map/ppermute | solution.py:205
  4.4 1.2 %collective-permute-done = f32[32,2304]{1,0:T(8,128)S(1)} collective-permute-done((f32[32,2304]{1,0:T(8,128)S(1)}, f32[32,2304]{1,0:T(8,128)S(1)}, u32[]{:S(2)}, u32[]{:S(2)}) %collective-permute-start) | collective-permute-done | bytes 294944 | tf_op jit(solution)/shard_map/ppermute | solution.py:205
  5.7 2.7 %collective-permute-start.1 = (f32[8,2304]{1,0:T(8,128)S(1)}, f32[8,2304]{1,0:T(8,128)S(1)}, u32[]{:S(2)}, u32[]{:S(2)}) collective-permute-start(f32[8,2304]{1,0:T(8,128)S(1)} %get-tuple-element.9), channel_id=1, source_target_pairs={{0,3},{1,2},{2,1},{3,0},{4,7},{5,6},{6,5},{7,4},{8,11},{9,10},{10,... | collective-permute-start | bytes 221192 | tf_op jit(solution)/shard_map/ppermute | solution.py:205
  8.4 1.5 %collective-permute-start.3 = (f32[8,2304]{1,0:T(8,128)S(1)}, f32[8,2304]{1,0:T(8,128)S(1)}, u32[]{:S(2)}, u32[]{:S(2)}) collective-permute-start(f32[8,2304]{1,0:T(8,128)S(1)} %get-tuple-element.10), channel_id=1, source_target_pairs={{0,6},{1,7},{2,4},{3,5},{4,2},{5,3},{6,0},{7,1},{8,14},{9,15},{10,... | collective-permute-start | bytes 221192 | tf_op jit(solution)/shard_map/ppermute | solution.py:205
  9.9 0.0 collective-permute-start.2
  9.9 2.4 %collective-permute-done.1 = f32[8,2304]{1,0:T(8,128)S(1)} collective-permute-done((f32[8,2304]{1,0:T(8,128)S(1)}, f32[8,2304]{1,0:T(8,128)S(1)}, u32[]{:S(2)}, u32[]{:S(2)}) %collective-permute-start.1) | collective-permute-done | bytes 73760 | tf_op jit(solution)/shard_map/ppermute | solution.py:205
  12.3 1.5 %collective-permute-done.3 = f32[8,2304]{1,0:T(8,128)S(1)} collective-permute-done((f32[8,2304]{1,0:T(8,128)S(1)}, f32[8,2304]{1,0:T(8,128)S(1)}, u32[]{:S(2)}, u32[]{:S(2)}) %collective-permute-start.3) | collective-permute-done | bytes 73760 | tf_op jit(solution)/shard_map/ppermute | solution.py:205
  13.8 0.4 %collective-permute-done.2 = f32[8,2304]{1,0:T(8,128)S(1)} collective-permute-done((f32[8,2304]{1,0:T(8,128)S(1)}, f32[8,2304]{1,0:T(8,128)S(1)}, u32[]{:S(2)}, u32[]{:S(2)}) %collective-permute-start.2) | collective-permute-done | bytes 73760 | tf_op jit(solution)/shard_map/ppermute | solution.py:205
  14.2 2.4 %collective-permute-start.4 = (f32[4,2304]{1,0:T(4,128)S(1)}, f32[4,2304]{1,0:T(4,128)S(1)}, u32[]{:S(2)}, u32[]{:S(2)}) collective-permute-start(f32[4,2304]{1,0:T(4,128)S(1)} %slice.24), channel_id=1, source_target_pairs={{0,9},{1,8},{2,11},{3,10},{4,13},{5,12},{6,15},{7,14},{8,1},{9,0},... | collective-permute-start | bytes 110600 | tf_op jit(solution)/shard_map/ppermute | solution.py:205
  16.6 2.0 %collective-permute-done.4.second_ref = f32[4,2304]{1,0:T(4,128)S(1)} collective-permute-done((f32[4,2304]{1,0:T(4,128)S(1)}, f32[4,2304]{1,0:T(4,128)S(1)}, u32[]{:S(2)}, u32[]{:S(2)}) %collective-permute-start.4) | collective-permute-done | bytes 36896 | tf_op jit(solution)/shard_map/ppermute | solution.py:205
  18.7 0.9 %expand.1 = f32[4,4096]{1,0:T(4,128)} custom-call(f32[8,2304]{1,0:T(8,128)S(1)} %fusion.1.first_ref, f32[4,2304]{1,0:T(4,128)S(1)} %collective-permute-done.4.second_ref), custom_call_target="tpu_custom_call" | custom-call | tf_op jit(solution)/shard_map/expand/pallas_call | solution.py:220
  (4 shorter events, 0.1 us)
Async XLA Ops:
  3.9 1.7 %collective-permute-start = (f32[32,2304]{1,0:T(8,128)S(1)}, f32[32,2304]{1,0:T(8,128)S(1)}, u32[]{:S(2)}, u32[]{:S(2)}) collective-permute-start(f32[32,2304]{1,0:T(8,128)S(1)} %get-tuple-element.8), channel_id=1, source_target_pairs={{0,1},{1,0},{2,3},{3,2},{4,5},{5,4},{6,7},{7,6},{8,9},{9,8},{10,11... | collective-permute-start | bytes 884744 | tf_op jit(solution)/shard_map/ppermute | solution.py:205
  5.7 6.7 %collective-permute-start.1 = (f32[8,2304]{1,0:T(8,128)S(1)}, f32[8,2304]{1,0:T(8,128)S(1)}, u32[]{:S(2)}, u32[]{:S(2)}) collective-permute-start(f32[8,2304]{1,0:T(8,128)S(1)} %get-tuple-element.9), channel_id=1, source_target_pairs={{0,3},{1,2},{2,1},{3,0},{4,7},{5,6},{6,5},{7,4},{8,11},{9,10},{10,... | collective-permute-start | bytes 221192 | tf_op jit(solution)/shard_map/ppermute | solution.py:205
  8.4 5.4 %collective-permute-start.3 = (f32[8,2304]{1,0:T(8,128)S(1)}, f32[8,2304]{1,0:T(8,128)S(1)}, u32[]{:S(2)}, u32[]{:S(2)}) collective-permute-start(f32[8,2304]{1,0:T(8,128)S(1)} %get-tuple-element.10), channel_id=1, source_target_pairs={{0,6},{1,7},{2,4},{3,5},{4,2},{5,3},{6,0},{7,1},{8,14},{9,15},{10,... | collective-permute-start | bytes 221192 | tf_op jit(solution)/shard_map/ppermute | solution.py:205
  9.9 4.3 %collective-permute-start.2 = (f32[8,2304]{1,0:T(8,128)S(1)}, f32[8,2304]{1,0:T(8,128)S(1)}, u32[]{:S(2)}, u32[]{:S(2)}) collective-permute-start(f32[8,2304]{1,0:T(8,128)S(1)} %get-tuple-element.11), channel_id=1, source_target_pairs={{0,5},{1,4},{2,7},{3,6},{4,1},{5,0},{6,3},{7,2},{8,13},{9,12},{10,... | collective-permute-start | bytes 221192 | tf_op jit(solution)/shard_map/ppermute | solution.py:205
  14.2 4.4 %collective-permute-start.4 = (f32[4,2304]{1,0:T(4,128)S(1)}, f32[4,2304]{1,0:T(4,128)S(1)}, u32[]{:S(2)}, u32[]{:S(2)}) collective-permute-start(f32[4,2304]{1,0:T(4,128)S(1)} %slice.24), channel_id=1, source_target_pairs={{0,9},{1,8},{2,11},{3,10},{4,13},{5,12},{6,15},{7,14},{8,1},{9,0},... | collective-permute-start | bytes 110600 | tf_op jit(solution)/shard_map/ppermute | solution.py:205
